TPU v7x, 32 devices: a whole 2x2x4 slice. The times are simulated.
32 devices in a mesh: groups: 2 (over y), expert: 8 (over z, core), helper: 2 (over x), dp: 1.
Axes of the slice: x: 2, y: 2, z: 4, core: 2. Of those that a mesh axis runs over, the one named last changes fastest.
Arguments:
- tokens: bfloat16 [2048, 2048], P(('groups', 'expert', 'dp')), parts along dimension 0, may hold values from -6 to 6
- expert_ids: int32 [2048, 4], P(('groups', 'expert', 'dp')), parts along dimension 0, may hold values from 0 to 7, all different within a row; in each aligned block of 128 rows (0 to 127, 128 to 255, ...) at most 80 rows name the same one
- pick_counts: int32 [2048], P(('groups', 'expert', 'dp')), parts along dimension 0, may hold values from 1 to 4
- gate_scores: float32 [2048, 4], P(('groups', 'expert', 'dp')), parts along dimension 0, may hold values from 0.05 to 1
- w_gate: bfloat16 [8, 2048, 2048], P('expert', None, 'helper'), may hold values from -0.125 to 0.125
- w_up: bfloat16 [8, 2048, 2048], P('expert', None, 'helper'), may hold values from -0.125 to 0.125
- w_down: bfloat16 [8, 2048, 2048], P('expert', 'helper'), may hold values from -0.125 to 0.125
- grad_out: bfloat16 [2048, 2048], P(('groups', 'expert', 'dp')), parts along dimension 0, may hold values from -6 to 6
Outputs:
- outputs: bfloat16 [2048, 2048], P(('groups', 'expert', 'dp'), 'helper'), parts along dimension 0
- input_grads: bfloat16 [2048, 2048], P(('groups', 'expert', 'dp'), 'helper'), parts along dimension 0
- d_scores: float32 [2048, 4], P(('groups', 'expert', 'dp')), parts along dimension 0
- grad_w_gate: bfloat16 [16, 2048, 2048], P(('groups', 'expert'), 'dp', 'helper'), parts along dimension 0
- grad_w_up: bfloat16 [16, 2048, 2048], P(('groups', 'expert'), 'dp', 'helper'), parts along dimension 0
- grad_w_down: bfloat16 [16, 2048, 2048], P(('groups', 'expert'), 'helper', 'dp'), parts along dimension 0
There are 2 independent parts, one for each index of `groups`. A program takes and returns all parts, laid end to end along the dimension named above; an argument that names none is the same for every part. Nothing has to cross between parts.
Inputs may be any that keep to these rules, and one draw needn't show every extreme that they name: `expert_ids`: in each aligned block of 128 rows (the rows of one device), no expert is named by more than 80 rows over all 4 columns; the entries of a row are distinct.
All inputs are finite; a program needn't handle non-finite values.
Results may differ from a plain program's by a relative error of at most 0.015.
Values may be sent and summed in bfloat16 or wider, within the bound.
No kernel may reach another device: no remote copies, remote signals or barrier semaphores. Data moves between devices by JAX's collectives and lax.ppermute only.
A program may use at most 128 MiB of HBM per device.

v0:
```python
import functools

import jax
import jax.numpy as jnp
from jax import lax
from jax.experimental import pallas as pl
from jax.experimental.pallas import tpu as pltpu
from jax.sharding import PartitionSpec as P

LANES = 128
VMEM = pl.BlockSpec(memory_space=pltpu.VMEM)


def product(first_mat, second_mat):
    return jnp.dot(first_mat, second_mat, preferred_element_type=jnp.float32)


def transposed_product(first_mat, second_mat):
    return lax.dot_general(
        first_mat, second_mat, (((0,), (0,)), ((), ())), preferred_element_type=jnp.float32
    )


def right_transposed(first_mat, second_mat):
    return lax.dot_general(
        first_mat, second_mat, (((1,), (1,)), ((), ())), preferred_element_type=jnp.float32
    )


def silu_parts(argument):
    sigmoid_part = jax.nn.sigmoid(argument)
    return argument * sigmoid_part, sigmoid_part * (1.0 + argument * (1.0 - sigmoid_part))


def total_of(terms):
    return functools.reduce(jnp.add, terms)


def call(kernel, name, operands, out_shape, scratch=(), flops=0, moved=0, mebibytes=12):
    return pl.pallas_call(
        kernel,
        out_shape=out_shape,
        in_specs=[VMEM] * len(operands),
        out_specs=jax.tree.map(lambda _: VMEM, out_shape),
        scratch_shapes=scratch,
        compiler_params=pltpu.CompilerParams(vmem_limit_bytes=mebibytes * 2**20),
        cost_estimate=pl.CostEstimate(
            flops=flops, bytes_accessed=moved, transcendentals=0
        ),
        name=name,
    )(*operands)


def half_at(array, which):
    rows = array.shape[0] // 2
    return array[which * rows : (which + 1) * rows]


def swap_halves(array):
    return jnp.concatenate([half_at(array, 1), half_at(array, 0)], axis=0)


def hi_lo(values, is_high):
    high = values.astype(jnp.bfloat16).astype(jnp.float32)
    return jnp.where(is_high, high, values - high).astype(jnp.bfloat16)


def gate_rows(counts, scores):
    used = [(counts > k).astype(jnp.float32) for k in range(scores.shape[0])]
    weighted = [scores[k : k + 1] * used[k] for k in range(scores.shape[0])]
    score_sum = total_of(weighted)
    return [w / score_sum for w in weighted], used, score_sum


def prepare_rows_kernel(experts, *refs):
    sources, (own, pair, clock), targets, sems = refs[:4], refs[4:7], refs[7:11], refs[11]
    ids, counts, scores, rows = targets
    copies = [
        pltpu.make_async_copy(source, target, sems.at[i])
        for i, (source, target) in enumerate(zip(sources, targets))
    ]
    for copy in copies:
        copy.start()
    for copy in copies:
        copy.wait()
    total, width = rows.shape
    clock[...] = jnp.zeros_like(clock)
    lane = lax.broadcasted_iota(jnp.int32, (LANES, total), 0)
    gates, _, _ = gate_rows(counts[...], scores[...])
    table = jnp.zeros((LANES, total), jnp.float32)
    for k, gate in enumerate(gates):
        named = ids[k : k + 1, :]
        table = table + jnp.where((lane == named) | (lane == named + experts), gate, 0.0)
    table = table.T
    table = hi_lo(table, lax.broadcasted_iota(jnp.int32, table.shape, 1) < experts)
    for side in range(2):

        @pl.when(lax.axis_index("helper") == side)
        def _(side=side):
            own[:, :width] = half_at(rows, side)
            own[:, width:] = half_at(table, side)
            for i, which in enumerate((side, 1 - side)):
                here = slice(i * total // 2, (i + 1) * total // 2)
                pair[here, :width] = half_at(rows, which)
                pair[here, width:] = half_at(table, which)


def prepare_rows(ids, counts, scores, rows, experts):
    total, width = rows.shape
    piece = jax.ShapeDtypeStruct((total // 2, width + LANES), jnp.bfloat16)
    operands = (ids, counts, scores, rows)
    return pl.pallas_call(
        functools.partial(prepare_rows_kernel, experts),
        out_shape=(
            piece,
            jax.ShapeDtypeStruct((total, width + LANES), jnp.bfloat16),
            jax.ShapeDtypeStruct((8, LANES), jnp.float32),
        ),
        in_specs=[pl.BlockSpec(memory_space=pltpu.HBM)] * len(operands),
        out_specs=(VMEM,) * 3,
        scratch_shapes=[
            *(pltpu.VMEM(operand.shape, operand.dtype) for operand in operands),
            pltpu.SemaphoreType.DMA((len(operands),)),
        ],
        compiler_params=pltpu.CompilerParams(vmem_limit_bytes=8 * 2**20),
        name="prepare_rows",
    )(*(pltpu.with_memory_space_constraint(operand, pltpu.HBM) for operand in operands))


def prepare_grads_kernel(rows, own, pair):
    half = rows.shape[0] // 2
    for side in range(2):

        @pl.when(lax.axis_index("helper") == side)
        def _(side=side):
            own[...] = half_at(rows, side)
            pair[:half, :] = half_at(rows, side)
            pair[half:, :] = half_at(rows, 1 - side)


def prepare_grads(rows):
    total, width = rows.shape
    piece = jax.ShapeDtypeStruct((total // 2, width), jnp.bfloat16)
    return call(
        prepare_grads_kernel,
        "prepare_grads",
        (rows,),
        (piece, jax.ShapeDtypeStruct(rows.shape, jnp.bfloat16)),
    )


def join_kernel(starts, rows, *refs):
    for i, start in enumerate(starts):
        refs[-1][i * rows : (i + 1) * rows, :] = refs[i][start : start + rows, :]


def join(rows, pieces, starts):
    shape = jax.ShapeDtypeStruct((len(pieces) * rows, pieces[0].shape[1]), pieces[0].dtype)
    return call(functools.partial(join_kernel, starts, rows), "join", pieces, shape)


def parts_of(pair, rest):
    rows = pair.shape[0]
    half = rows // 2
    parts = [(pair, 0, rows)]
    for slot in range(2):
        parts = parts + [(rest, slot * half, half), (rest, rows + slot * half, half)]
    return parts + [(rest, 2 * rows, rows)]


def lay_out(pieces, target, columns, at=0):
    for piece, start, rows in parts_of(*pieces):
        target[at : at + rows, :] = piece[start : start + rows, columns]
        at = at + rows


def gate_column(experts, pieces, width):
    table = jnp.concatenate(
        [piece[start : start + rows, width:] for piece, start, rows in parts_of(*pieces)], axis=0
    )
    lane = lax.broadcasted_iota(jnp.int32, table.shape, 1)
    expert = lax.axis_index("expert")
    mine = (lane == expert) | (lane == expert + experts)
    return jnp.sum(jnp.where(mine, table.astype(jnp.float32), 0.0), axis=1, keepdims=True)


def hidden_kernel(experts, tile, *refs):
    pieces, refs = refs[:2], refs[2:]
    gate_mat, up_mat, pre_gate, pre_up, gated, rows = refs
    width = rows.shape[1]
    lay_out(pieces, rows, slice(0, width))
    gate = gate_column(experts, pieces, width)
    for start in range(0, gated.shape[1], tile):
        columns = slice(start, start + tile)
        gate_part = product(rows[...], gate_mat[:, columns])
        up_part = product(rows[...], up_mat[:, columns])
        silu_value, _ = silu_parts(gate_part)
        pre_gate[:, columns] = gate_part
        pre_up[:, columns] = up_part
        gated[:, columns] = (gate * silu_value * up_part).astype(jnp.bfloat16)


def hidden_units(pieces, gate_mat, up_mat, experts):
    width, hidden = gate_mat.shape
    total = 4 * pieces[0].shape[0]
    pre = jax.ShapeDtypeStruct((total, hidden), jnp.float32)
    act = jax.ShapeDtypeStruct((total, hidden), jnp.bfloat16)
    return call(
        functools.partial(hidden_kernel, experts, 256),
        "hidden_units",
        (*pieces, gate_mat, up_mat),
        (pre, pre, act),
        [pltpu.VMEM((total, width), jnp.bfloat16)],
        flops=4 * total * width * hidden,
        mebibytes=12,
    )


def outputs_kernel(tile, gated, down_mat, *sums):
    half = sums[0].shape[1]
    for keep in range(2):
        side = lax.axis_index("helper")
        side = side if keep else 1 - side
        for start in range(0, half, tile):
            here = pl.ds(pl.multiple_of(side * half + start, tile), tile)
            out = product(gated[...], down_mat[:, here])
            sums[keep][:, start : start + tile] = out.astype(jnp.bfloat16)


def outputs_of(gated, down_mat):
    total, hidden = gated.shape
    width = down_mat.shape[1]
    sums = jax.ShapeDtypeStruct((total, width // 2), jnp.bfloat16)
    return call(
        functools.partial(outputs_kernel, 256), "outputs", (gated, down_mat), (sums, sums)
    )


def hidden_grads_kernel(experts, tile, *refs):
    pieces, gate_pieces, refs = refs[:2], refs[2:4], refs[4:]
    down_mat, pre_gate, pre_up, d_gate, d_up, shares_out, grads = refs
    total, width = grads.shape
    lay_out(pieces, grads, slice(0, width))
    gate = gate_column(experts, gate_pieces, width)
    shares = []
    for start in range(0, d_gate.shape[1], tile):
        columns = slice(start, start + tile)
        raw = right_transposed(grads[...], down_mat[columns, :])
        up_part = pre_up[:, columns]
        silu_value, silu_slope = silu_parts(pre_gate[:, columns])
        share = raw * silu_value * up_part
        shares = shares + [share[:, c : c + LANES] for c in range(0, tile, LANES)]
        d_act = gate * raw
        d_gate[:, columns] = (d_act * up_part * silu_slope).astype(jnp.bfloat16)
        d_up[:, columns] = (d_act * silu_value).astype(jnp.bfloat16)
    value = jnp.sum(total_of(shares), axis=1, keepdims=True)
    lane = lax.broadcasted_iota(jnp.int32, (total, LANES), 1)
    high = 2 * lax.axis_index("expert") + lax.axis_index("helper")
    value = jnp.where((lane == high) | (lane == high + 2 * experts), value, 0.0)
    shares_out[...] = hi_lo(value, lane < 2 * experts)


def hidden_grads(pieces, gate_pieces, pre_gate, pre_up, down_mat, experts):
    hidden, width = down_mat.shape
    total = pre_gate.shape[0]
    act = jax.ShapeDtypeStruct((total, hidden), jnp.bfloat16)
    return call(
        functools.partial(hidden_grads_kernel, experts, 256),
        "hidden_grads",
        (*pieces, *gate_pieces, down_mat, pre_gate, pre_up),
        (act, act, jax.ShapeDtypeStruct((total, LANES), jnp.bfloat16)),
        [pltpu.VMEM((total, width), jnp.bfloat16)],
        mebibytes=12,
    )


def input_grads_kernel(tile, d_gate, d_up, shares, gate_mat, up_mat, *sums):
    half = sums[0].shape[1] - LANES
    split = len(sums) // 2

    def put(keep, columns, values):
        rows = values.shape[0] // split
        for i in range(split):
            sums[split * keep + i][:, columns] = values[i * rows : (i + 1) * rows]

    for keep in range(2):
        put(keep, slice(half, half + LANES), shares[...])
        side = lax.axis_index("helper")
        side = side if keep else 1 - side
        for start in range(0, half, tile):
            here = pl.ds(pl.multiple_of(side * half + start, tile), tile)
            back = right_transposed(d_gate[...], gate_mat[here, :])
            back = back + right_transposed(d_up[...], up_mat[here, :])
            put(keep, slice(start, start + tile), back.astype(jnp.bfloat16))


def input_grads_of(split, d_gate, d_up, shares, gate_mat, up_mat):
    width, hidden = gate_mat.shape
    total = d_gate.shape[0]
    sums = jax.ShapeDtypeStruct((total // split, width // 2 + LANES), jnp.bfloat16)
    return call(
        functools.partial(input_grads_kernel, 256),
        "input_grads",
        (d_gate, d_up, shares, gate_mat, up_mat),
        (sums,) * (2 * split),
        mebibytes=12,
    )


def weights_kernel(width, tile, *refs):
    pieces, (first, second, grad, rows, acts, made, sems) = refs[:4], refs[4:]
    total = first.shape[0]
    lay_out(pieces[:2], rows, slice(0, width))
    lay_out(pieces[2:], rows, slice(0, width), total)
    acts[:total, :] = first[...]
    acts[total:, :] = second[...]
    left, right = (acts, rows) if grad.shape[1] == width else (rows, acts)

    def copy(step):
        here = pl.ds(pl.multiple_of(step * tile, tile), tile)
        return pltpu.make_async_copy(made.at[here, :], grad.at[here, :], sems.at[step])

    steps = grad.shape[0] // tile

    @pl.loop(0, steps, unroll=2)
    def _(step):
        here = pl.ds(pl.multiple_of(step * tile, tile), tile)
        made[here, :] = transposed_product(left[:, here], right[...]).astype(jnp.bfloat16)
        copy(step).start()

    @pl.loop(0, steps)
    def _(step):
        copy(step).wait()


def weights(name, pieces, acts, width, by_hidden):
    rows, hidden = acts[0].shape
    shape = (hidden, width) if by_hidden else (width, hidden)
    operands = (*pieces, *acts)
    return pl.pallas_call(
        functools.partial(weights_kernel, width, 512),
        out_shape=jax.ShapeDtypeStruct(shape, jnp.bfloat16),
        in_specs=[VMEM] * len(operands),
        out_specs=pl.BlockSpec(memory_space=pl.ANY),
        scratch_shapes=[
            pltpu.VMEM((2 * rows, width), jnp.bfloat16),
            pltpu.VMEM((2 * rows, hidden), jnp.bfloat16),
            pltpu.VMEM(shape, jnp.bfloat16),
            pltpu.SemaphoreType.DMA((shape[0] // 512,)),
        ],
        compiler_params=pltpu.CompilerParams(vmem_limit_bytes=16 * 2**20),
        cost_estimate=pl.CostEstimate(
            flops=4 * rows * width * hidden, bytes_accessed=0, transcendentals=0
        ),
        name=name,
    )(*operands)


def send_kernel(first, own, received, *sent):
    at = 0
    for target in sent:
        rows = target.shape[0]
        here = slice(first + at, first + at + rows)
        target[...] = own[here, :] + received[at : at + rows, :]
        at = at + rows


def slot_sum(own, received, arrived, slot, offset, received_slot):
    rows = LANES
    half = rows // 2
    here = slice(slot * rows, (slot + 1) * rows)
    other = arrived[offset : offset + rows, :].astype(jnp.float32)
    there = slice(received_slot * rows, (received_slot + 1) * rows)
    kept = own[here, :].astype(jnp.float32) + received[there, :].astype(jnp.float32)
    return kept + jnp.concatenate([other[half:], other[:half]], axis=0)


def slots_kernel(own, received, arrived, near_and_last, far_slot):
    rows = far_slot.shape[0]
    targets = (near_and_last.at[:rows], far_slot, near_and_last.at[rows:])
    for i, target in enumerate(targets):
        whole = slot_sum(own, received, arrived, i + 1, i * rows, i + 1)
        target[...] = whole.astype(target.dtype)


def add_last_kernel(far_slot, arrived, total):
    rows = far_slot.shape[0]
    total[...] = far_slot[...] + arrived[rows:, :]


def slot_kernel(slot, own, received, arrived, *refs):
    whole = slot_sum(own, received, arrived, slot, 0, slot % 2)
    if len(refs) > 1:
        whole = whole + refs[0][...].astype(jnp.float32)
    refs[-1][...] = whole.astype(refs[-1].dtype)


def finish_outputs_kernel(own, received, arrived, near_and_last, far, columns):
    near = near_and_last[: far.shape[0], :]
    whole = slot_sum(own, received, arrived, 0, 0, 0)
    whole = total_of([whole, near.astype(jnp.float32), far[...].astype(jnp.float32)])
    whole = jnp.where(lax.axis_index("helper") == 0, whole, swap_halves(whole))
    columns[...] = whole.astype(jnp.bfloat16)


def finish_inputs_kernel(experts, ids, counts, scores, clock, own, received, arrived, *refs):
    columns, d_scores = refs[-2:]
    width = columns.shape[1]
    whole = slot_sum(own, received, arrived, 0, 0, 0)
    whole = total_of([whole] + [ref[...].astype(jnp.float32) for ref in refs[:-2]])
    whole = jnp.where(lax.axis_index("helper") == 0, whole, swap_halves(whole))
    columns[...] = whole[:, :width].astype(jnp.bfloat16)
    table = whole[:, width:].T
    lane = lax.broadcasted_iota(jnp.int32, table.shape, 0)
    named_by = (lane % (2 * experts)) // 2
    gates, used, score_sum = gate_rows(counts[...], scores[...])
    d_gates = []
    for k in range(len(gates)):
        hit = (named_by == ids[k : k + 1, :]) & (lane < 4 * experts)
        d_gates.append(jnp.sum(jnp.where(hit, table, 0.0), axis=0, keepdims=True))
    mean = total_of([gate * d_gate for gate, d_gate in zip(gates, d_gates)])
    for k, d_gate in enumerate(d_gates):
        d_scores[k : k + 1, :] = used[k] * (d_gate - mean) / score_sum


class FourChips:
    def __init__(self, label):
        self.label = label
        both = lambda pairs: [(2 * a + c, 2 * b + c) for a, b in pairs for c in (0, 1)]
        self.near = both([(z, z ^ 1) for z in range(4)])
        self.far = both([(z, z ^ 2) for z in range(4)])
        self.cores = [(i, i ^ 1) for i in range(8)]
        self.sides = [(0, 1), (1, 0)]

    def line(self, array, pairs):
        with jax.named_scope(self.label + "_line"):
            return lax.ppermute(array, "expert", pairs)

    def sibling(self, array):
        with jax.named_scope(self.label + "_cores"):
            return lax.ppermute(array, "expert", self.cores)

    def across(self, array):
        with jax.named_scope(self.label + "_across"):
            return lax.ppermute(array, "helper", self.sides)

    def send(self, first, own, received, parts):
        shape = lambda rows: jax.ShapeDtypeStruct((rows, received.shape[1]), own.dtype)
        return call(
            functools.partial(send_kernel, first),
            self.label + "_send",
            (own, received),
            tuple(shape(rows) for rows in parts),
        )

    def slots(self, own, received, arrived):
        rows, columns = arrived.shape
        shape = lambda slots: jax.ShapeDtypeStruct((slots * rows // 3, columns), arrived.dtype)
        return call(
            slots_kernel,
            self.label + "_slots",
            (own, received, arrived),
            (shape(2), shape(1)),
        )

    def slot(self, which, own, received, arrived, *others):
        return call(
            functools.partial(slot_kernel, which),
            self.label + "_slot",
            (own, received, arrived, *others),
            jax.ShapeDtypeStruct(arrived.shape, arrived.dtype),
        )


def load_kernel(*refs):
    sources, targets, sems = refs[:3], refs[3:6], refs[6]
    copies = [
        pltpu.make_async_copy(source, target, sems.at[i])
        for i, (source, target) in enumerate(zip(sources, targets))
    ]
    for copy in copies:
        copy.start()
    for copy in copies:
        copy.wait()


def load(*mats):
    return pl.pallas_call(
        load_kernel,
        out_shape=tuple(jax.ShapeDtypeStruct(mat.shape, mat.dtype) for mat in mats),
        in_specs=[pl.BlockSpec(memory_space=pltpu.HBM)] * len(mats),
        out_specs=(VMEM,) * len(mats),
        scratch_shapes=[pltpu.SemaphoreType.DMA((len(mats),))],
        compiler_params=pltpu.CompilerParams(vmem_limit_bytes=2**20),
        name="load",
    )(*(pltpu.with_memory_space_constraint(mat, pltpu.HBM) for mat in mats))


def space(clock, flops=36 * 10**9):
    return pl.pallas_call(
        lambda old, new: None,
        out_shape=jax.ShapeDtypeStruct(clock.shape, clock.dtype),
        in_specs=[pl.BlockSpec(memory_space=pl.ANY)],
        out_specs=pl.BlockSpec(memory_space=pl.ANY),
        input_output_aliases={0: 0},
        compiler_params=pltpu.CompilerParams(vmem_limit_bytes=2**20),
        cost_estimate=pl.CostEstimate(flops=flops, bytes_accessed=0, transcendentals=0),
        name="space",
    )(clock)


class Order:
    def __init__(self):
        self.token = None

    def __call__(self, function, *operands, also=()):
        if self.token is not None:
            operands, _ = lax.optimization_barrier((operands, (self.token, also)))
        result = function(*operands)
        self.token = result
        return result


def lined_up(tokens, expert_ids, pick_counts, gate_scores, gate_local, up_local, down_local, grad_out):
    experts = lax.axis_size("expert")
    width = gate_local.shape[0]
    picks = (expert_ids.T, pick_counts[None, :], gate_scores.T)
    rows, grads, outs, ins = (FourChips(label) for label in ("rows", "grads", "out", "in"))
    order = Order()
    hold = lambda value, *tokens: lax.optimization_barrier((value, tokens))[0]
    product_of = lambda name, by_hidden: lambda r, acts: weights(name, r, acts, width, by_hidden)

    size = tokens.shape[0]
    half = size // 2
    zeros = (0,) * 6
    own, pair, clock = order(lambda r: prepare_rows(*picks, r, experts), tokens)
    near = rows.line(own, rows.near)
    far = rows.line(own, rows.far)
    sibling_pair = rows.sibling(pair)
    gate_mat, up_mat, down_mat = order(load, gate_local, up_local, down_local)
    sibling_pair = hold(sibling_pair, down_mat)
    line_pair = order(lambda *p: join(half, p, zeros[:2]), near, far, also=sibling_pair)
    last = rows.line(hold(far, line_pair), rows.near)
    across_pair = rows.across(line_pair)
    own, grads_pair = order(prepare_grads, grad_out)
    far = grads.line(own, grads.far)
    last_across = rows.across(last)
    far = hold(far, last)
    grads_last = grads.line(far, grads.near)
    far_across = grads.across(far)
    near = grads.line(hold(grads_pair, last), grads.near)
    clock = order(lambda c: space(c, 2 * 10**9), clock, also=far)
    across_pair, last_across = hold((across_pair, last_across), clock)
    rest = order(
        lambda *p: join(half, p, (0, half, 0, half, 0, 0)),
        line_pair,
        line_pair,
        across_pair,
        across_pair,
        last,
        last_across,
    )
    own_rows = (pair, rest)
    sibling_rest = rows.sibling(rest)
    clock = order(space, clock)
    other_rows = (sibling_pair, hold(sibling_rest, clock))
    hidden = lambda *r: hidden_units(r, gate_mat, up_mat, experts)
    own_gate, own_up, own_act = order(hidden, *own_rows)
    grads_last, far_across = hold((grads_last, far_across), own_act)
    last_across = grads.across(grads_last)
    grads_sibling = grads.sibling(hold(grads_pair, own_act))
    other_gate, other_up, other_act = order(hidden, *other_rows, also=(grads_last, far_across))
    sent, kept = order(outputs_of, other_act, down_mat)
    received, kept = outs.sibling(sent), outs.sibling(kept)
    out_send, out_keep = order(outputs_of, own_act, down_mat)
    clock = order(space, clock, also=(near, last_across, grads_sibling))
    received = hold(received, clock)
    out_sent, sent = order(
        lambda *s: outs.send(0, *s, (size, 3 * size)), out_send, received
    )
    arrived = outs.across(sent)
    rest = order(
        lambda *p: join(half, p, (0, 0, half, 0, 0, 0)),
        near,
        far,
        near,
        far_across,
        grads_last,
        last_across,
    )
    own_grads = (grads_pair, rest)
    other_grads = (grads_sibling, grads.sibling(rest))
    back = lambda g, r, *pre: hidden_grads(g, r, *pre, down_mat, experts)
    own_d_gate, own_d_up, own_shares = order(back, own_grads, own_rows, own_gate, own_up)
    other_d_gate, other_d_up, other_shares = order(
        back, other_grads, other_rows, other_gate, other_up
    )
    near_sent, far_sent, near_kept, far_kept = order(
        lambda *d: input_grads_of(2, *d, gate_mat, up_mat), other_d_gate, other_d_up, other_shares
    )
    far_received, far_kept = ins.sibling(far_sent), ins.sibling(far_kept)
    near_received, near_kept = ins.sibling(near_sent), ins.sibling(near_kept)
    in_send, in_keep = order(
        lambda *d: input_grads_of(1, *d, gate_mat, up_mat), own_d_gate, own_d_up, own_shares
    )
    far_sent, last_sent = order(
        lambda *s: ins.send(2 * size, *s, (size, size)), in_send, far_received
    )
    last_arrived = ins.across(last_sent)
    near_slots, far_slot = order(outs.slots, out_keep, kept, hold(arrived, far_sent))
    near_sums = outs.line(near_slots, outs.near)
    grad_down = order(product_of("grad_down", True), own_grads + other_grads, (own_act, other_act))
    slot = order(lambda *s: ins.slot(3, *s), in_keep, far_kept, last_arrived)
    last_sum = ins.line(slot, ins.near)
    far_arrived = ins.across(hold(far_sent, slot))
    out_arrived = outs.across(hold(out_sent, slot))
    own_sent, near_sent = order(
        lambda *s: ins.send(0, *s, (size, size)), in_send, near_received
    )
    far_slot = order(
        lambda *s: call(add_last_kernel, "add_last", s, jax.ShapeDtypeStruct(s[0].shape, s[0].dtype)),
        far_slot,
        near_sums,
    )
    far_sum = outs.line(far_slot, outs.far)
    grad_gate = order(product_of("grad_gate", False), own_rows + other_rows, (own_d_gate, other_d_gate))
    slot = order(
        lambda *s: ins.slot(2, *s), in_keep, far_kept, far_arrived, last_sum, also=out_arrived
    )
    far = ins.line(slot, ins.far)
    near_arrived = ins.across(hold(near_sent, slot))
    grad_up = order(product_of("grad_up", False), own_rows + other_rows, (own_d_up, other_d_up))
    slot = order(lambda *s: ins.slot(1, *s), in_keep, near_kept, near_arrived)
    near = ins.line(slot, ins.near)
    own_arrived = ins.across(hold(own_sent, slot))
    columns = jax.ShapeDtypeStruct((size, width // 2), jnp.bfloat16)
    output_cols = order(
        lambda *sums: call(finish_outputs_kernel, "finish_outputs", sums, columns),
        out_keep,
        kept,
        out_arrived,
        near_sums,
        far_sum,
    )
    clock = order(lambda c: space(c, 2 * 10**9), clock, also=far)
    near, own_arrived = hold((near, own_arrived), clock)
    input_cols, d_scores = order(
        lambda *sums: call(
            functools.partial(finish_inputs_kernel, experts),
            "finish_inputs",
            (*picks, clock, *sums),
            (columns, jax.ShapeDtypeStruct(picks[2].shape, jnp.float32)),
        ),
        in_keep,
        near_kept,
        own_arrived,
        far,
        near,
    )
    return output_cols, input_cols, d_scores.T, grad_gate[None], grad_up[None], grad_down[None]


def any_mesh(tokens, expert_ids, pick_counts, gate_scores, gate_local, up_local, down_local, grad_out):
    tok_rows = tokens.shape[0]
    pick_width = expert_ids.shape[1]
    experts = lax.axis_size("expert")
    active_mask = lax.broadcasted_iota(jnp.int32, (tok_rows, pick_width), 1) < pick_counts[:, None]
    active_float = active_mask.astype(jnp.float32)
    weighted = gate_scores * active_float
    score_sum = jnp.sum(weighted, axis=1, keepdims=True)
    gate_weights = weighted / score_sum
    picked = (expert_ids[:, :, None] == lax.broadcasted_iota(jnp.int32, (1, 1, experts), 2)).astype(
        jnp.float32
    )
    gate_table = jnp.sum(gate_weights[:, :, None] * picked, axis=1)

    def combine(partial):
        summed = lax.psum_scatter(partial, "expert", scatter_dimension=0, tiled=True)
        return lax.psum_scatter(summed, "helper", scatter_dimension=1, tiled=True)

    rows = lax.all_gather(tokens, "expert", tiled=True)
    tables = lax.all_gather(gate_table.T, "expert", tiled=False)
    gates = jnp.take(tables, lax.axis_index("expert"), axis=1).reshape(-1, 1)
    grads = lax.all_gather(grad_out, "expert", tiled=True)

    pre_gate = product(rows, gate_local)
    pre_up = product(rows, up_local)
    silu_value, silu_slope = silu_parts(pre_gate)
    hidden_act = silu_value * pre_up
    gated_act = (gates * hidden_act).astype(jnp.bfloat16)
    output_cols = combine(product(gated_act, down_local).astype(jnp.bfloat16))

    raw_act = right_transposed(grads, down_local)
    gate_part = jnp.sum(raw_act * hidden_act, axis=1)
    d_act = gates * raw_act
    d_pre_gate = (d_act * pre_up * silu_slope).astype(jnp.bfloat16)
    d_pre_up = (d_act * silu_value).astype(jnp.bfloat16)
    input_cols = combine(
        (right_transposed(d_pre_gate, gate_local) + right_transposed(d_pre_up, up_local)).astype(
            jnp.bfloat16
        )
    )

    gate_parts = lax.all_gather(
        gate_part.reshape(-1, tok_rows), ("expert", "helper"), tiled=False
    )
    own_parts = jnp.take(gate_parts, lax.axis_index("expert"), axis=1)
    by_expert = jnp.sum(own_parts.reshape(experts, -1, tok_rows), axis=1).T
    d_gates = jnp.sum(by_expert[:, None, :] * picked, axis=2)
    d_scores = (
        active_float
        * (d_gates - jnp.sum(gate_weights * d_gates, axis=1, keepdims=True))
        / score_sum
    )

    def over_dp(whole, dimension):
        return lax.psum_scatter(
            whole.astype(jnp.bfloat16), "dp", scatter_dimension=dimension, tiled=True
        )[None]

    grad_w_gate = over_dp(transposed_product(rows, d_pre_gate), 0)
    grad_w_up = over_dp(transposed_product(rows, d_pre_up), 0)
    grad_w_down = over_dp(transposed_product(gated_act, grads), 1)
    return output_cols, input_cols, d_scores, grad_w_gate, grad_w_up, grad_w_down


def on_device(tokens, expert_ids, pick_counts, gate_scores, w_gate, w_up, w_down, grad_out):
    sizes = tuple(lax.axis_size(axis) for axis in ("expert", "helper", "dp"))
    layer = lined_up if sizes == (8, 2, 1) else any_mesh
    return layer(
        tokens, expert_ids, pick_counts, gate_scores, w_gate[0], w_up[0], w_down[0], grad_out
    )


def solution(mesh):
    in_specs = (
        P(("groups", "expert", "dp"), None),
        P(("groups", "expert", "dp"), None),
        P(("groups", "expert", "dp")),
        P(("groups", "expert", "dp"), None),
        P("expert", None, "helper"),
        P("expert", None, "helper"),
        P("expert", "helper", None),
        P(("groups", "expert", "dp"), None),
    )
    out_specs = (
        P(("groups", "expert", "dp"), "helper"),
        P(("groups", "expert", "dp"), "helper"),
        P(("groups", "expert", "dp"), None),
        P(("groups", "expert"), "dp", "helper"),
        P(("groups", "expert"), "dp", "helper"),
        P(("groups", "expert"), "helper", "dp"),
    )
    return jax.shard_map(
        on_device, mesh=mesh, in_specs=in_specs, out_specs=out_specs, check_vma=False
    )
```

profile of v0, /device:TPU:0, one launch (start us, length us, event | category | flops | bytes accessed | tf_op | source)
XLA Modules:
  0.0 128.0 jit_solution(2718064749887172058)
XLA Ops:
  0.6 1.3 %prepare_rows.1 = (bf16[64,2176]{1,0:T(8,128)(2,1)S(1)}, bf16[128,2176]{1,0:T(8,128)(2,1)S(1)}, f32[8,128]{1,0:T(8,128)S(1)}) custom-call(s32[4,128]{1,0:T(4,128)} %bitcast.10, s32[1,128]{1,0:T(1,128)} %bitcast.14, f32[4,128]{1,0:T(4,128)} %bitcast.12, bf16[128,2048]{1,0:T(8,128)(2,1)} %refs_3_.1), custom_call_target="tpu_custom_call" | custom-call | tf_op jit(solution)/shard_map/prepare_rows/pallas_call | solution.py:112
  1.9 0.5 collective-permute-start.2
  2.5 3.7 %collective-permute-start.1 = (bf16[64,2176]{1,0:T(8,128)(2,1)S(1)}, bf16[64,2176]{1,0:T(8,128)(2,1)S(1)}, u32[]{:S(2)}, u32[]{:S(2)}) collective-permute-start(bf16[64,2176]{1,0:T(8,128)(2,1)S(1)} %get-tuple-element.162), channel_id=1, source_target_pairs={{0,8},{2,10},{4,12},{6,14},{8,0},{10,2},{12,4},{14,6},{1,9},{3,11}... | collective-permute-start | bytes 835592 | tf_op jit(solution)/shard_map/rows_line/ppermute | solution.py:437
  6.1 1.6 %collective-permute-start = (bf16[64,2176]{1,0:T(8,128)(2,1)S(1)}, bf16[64,2176]{1,0:T(8,128)(2,1)S(1)}, u32[]{:S(2)}, u32[]{:S(2)}) collective-permute-start(bf16[64,2176]{1,0:T(8,128)(2,1)S(1)} %get-tuple-element.162), channel_id=1, source_target_pairs={{0,4},{2,6},{4,0},{6,2},{8,12},{10,14},{12,8},{14,10},{1,5},{3,7},... | collective-permute-start | bytes 835592 | tf_op jit(solution)/shard_map/rows_line/ppermute | solution.py:437
  7.7 4.7 %load.1 = (bf16[2048,1024]{1,0:T(8,128)(2,1)S(1)}, bf16[2048,1024]{1,0:T(8,128)(2,1)S(1)}, bf16[1024,2048]{1,0:T(8,128)(2,1)S(1)}) custom-call(bf16[2048,1024]{1,0:T(8,128)(2,1)} %bitcast.16, bf16[2048,1024]{1,0:T(8,128)(2,1)} %bitcast.17, bf16[1024,2048]{1,0:T(8,128)(2,1)} %bitcast.18), custom_call_target="tpu_custom_call" | custom-call | tf_op jit(solution)/shard_map/load/pallas_call | solution.py:488
  12.4 7.0 %collective-permute-done.1.refs_1_ = bf16[64,2176]{1,0:T(8,128)(2,1)S(1)} collective-permute-done((bf16[64,2176]{1,0:T(8,128)(2,1)S(1)}, bf16[64,2176]{1,0:T(8,128)(2,1)S(1)}, u32[]{:S(2)}, u32[]{:S(2)}) %collective-permute-start.1) | collective-permute-done | bytes 278560 | tf_op jit(solution)/shard_map/rows_line/ppermute | solution.py:437
  19.7 1.6 %collective-permute-start.4 = (bf16[64,2176]{1,0:T(8,128)(2,1)S(1)}, bf16[64,2176]{1,0:T(8,128)(2,1)S(1)}, u32[]{:S(2)}, u32[]{:S(2)}) collective-permute-start(bf16[64,2176]{1,0:T(8,128)(2,1)S(1)} %collective-permute-done.1.refs_1_), channel_id=1, source_target_pairs={{0,4},{2,6},{4,0},{6,2},{8,12},{10,14},{12,8},{14,10},{1,5},{3,7},... | collective-permute-start | bytes 835592 | tf_op jit(solution)/shard_map/rows_line/ppermute | solution.py:437
  21.2 1.5 %collective-permute-start.3 = (bf16[128,2176]{1,0:T(8,128)(2,1)S(1)}, bf16[128,2176]{1,0:T(8,128)(2,1)S(1)}, u32[]{:S(2)}, u32[]{:S(2)}) collective-permute-start(bf16[128,2176]{1,0:T(8,128)(2,1)S(1)} %join.3.refs_0_.refs_1_), channel_id=1, source_target_pairs={{0,1},{1,0},{2,3},{3,2},{4,5},{5,4},{6,7},{7,6},{8,9},{9,8},{10,11... | collective-permute-start | bytes 1671176 | tf_op jit(solution)/shard_map/rows_across/ppermute | solution.py:445
  22.8 2.4 %collective-permute-start.6 = (bf16[64,2048]{1,0:T(8,128)(2,1)S(1)}, bf16[64,2048]{1,0:T(8,128)(2,1)S(1)}, u32[]{:S(2)}, u32[]{:S(2)}) collective-permute-start(bf16[64,2048]{1,0:T(8,128)(2,1)S(1)} %get-tuple-element.175), channel_id=1, source_target_pairs={{0,8},{2,10},{4,12},{6,14},{8,0},{10,2},{12,4},{14,6},{1,9},{3,11}... | collective-permute-start | bytes 786440 | tf_op jit(solution)/shard_map/grads_line/ppermute | solution.py:437
  25.2 7.1 %collective-permute-done.4.refs_4_ = bf16[64,2176]{1,0:T(8,128)(2,1)S(1)} collective-permute-done((bf16[64,2176]{1,0:T(8,128)(2,1)S(1)}, bf16[64,2176]{1,0:T(8,128)(2,1)S(1)}, u32[]{:S(2)}, u32[]{:S(2)}) %collective-permute-start.4) | collective-permute-done | bytes 278560 | tf_op jit(solution)/shard_map/rows_line/ppermute | solution.py:437
  32.3 2.4 %collective-permute-start.5 = (bf16[64,2176]{1,0:T(8,128)(2,1)S(1)}, bf16[64,2176]{1,0:T(8,128)(2,1)S(1)}, u32[]{:S(2)}, u32[]{:S(2)}) collective-permute-start(bf16[64,2176]{1,0:T(8,128)(2,1)S(1)} %collective-permute-done.4.refs_4_), channel_id=1, source_target_pairs={{0,1},{1,0},{2,3},{3,2},{4,5},{5,4},{6,7},{7,6},{8,9},{9,8},{10,11... | collective-permute-start | bytes 835592 | tf_op jit(solution)/shard_map/rows_across/ppermute | solution.py:445
  34.7 2.2 %collective-permute-done.6.refs_1_ = bf16[64,2048]{1,0:T(8,128)(2,1)S(1)} collective-permute-done((bf16[64,2048]{1,0:T(8,128)(2,1)S(1)}, bf16[64,2048]{1,0:T(8,128)(2,1)S(1)}, u32[]{:S(2)}, u32[]{:S(2)}) %collective-permute-start.6) | collective-permute-done | bytes 262176 | tf_op jit(solution)/shard_map/grads_line/ppermute | solution.py:437
  36.9 0.5 collective-permute-start.9
  37.7 1.7 %collective-permute-start.12 = (bf16[128,2048]{1,0:T(8,128)(2,1)S(1)}, bf16[128,2048]{1,0:T(8,128)(2,1)S(1)}, u32[]{:S(2)}, u32[]{:S(2)}) collective-permute-start(bf16[128,2048]{1,0:T(8,128)(2,1)S(1)} %get-tuple-element.263.refs_0_), channel_id=1, source_target_pairs={{0,4},{2,6},{4,0},{6,2},{8,12},{10,14},{12,8},{14,10},{1,5},{3,7},... | collective-permute-start | bytes 1572872 | tf_op jit(solution)/shard_map/grads_line/ppermute | solution.py:437
  39.4 2.9 %collective-permute-done.5.refs_5_ = bf16[64,2176]{1,0:T(8,128)(2,1)S(1)} collective-permute-done((bf16[64,2176]{1,0:T(8,128)(2,1)S(1)}, bf16[64,2176]{1,0:T(8,128)(2,1)S(1)}, u32[]{:S(2)}, u32[]{:S(2)}) %collective-permute-start.5) | collective-permute-done | bytes 278560 | tf_op jit(solution)/shard_map/rows_across/ppermute | solution.py:445
  42.5 4.5 %hidden_units.2 = (f32[512,1024]{1,0:T(8,128)S(1)}, f32[512,1024]{1,0:T(8,128)S(1)}, bf16[512,1024]{1,0:T(8,128)(2,1)S(1)}) custom-call(bf16[128,2176]{1,0:T(8,128)(2,1)S(1)} %get-tuple-element.291.refs_0_.refs_2_, bf16[384,2176]{1,0:T(8,128)(2,1)S(1)} %join.4.refs_1_.refs_3_, bf16[2048,1024]{1,0:T(8,128)(2,1)S(1)} %get-tuple-element.167.refs_2_.gate_mat, ...), custom_call_target="tpu_custom_call" | custom-call | flops 4294967296 | tf_op jit(solution)/shard_map/hidden_units/pallas_call | solution.py:40
  47.0 0.6 collective-permute-start.14
  47.5 2.0 %collective-permute-start.13 = (bf16[64,2048]{1,0:T(8,128)(2,1)S(1)}, bf16[64,2048]{1,0:T(8,128)(2,1)S(1)}, u32[]{:S(2)}, u32[]{:S(2)}) collective-permute-start(bf16[64,2048]{1,0:T(8,128)(2,1)S(1)} %collective-permute-done.8.refs_4_), channel_id=1, source_target_pairs={{0,1},{1,0},{2,3},{3,2},{4,5},{5,4},{6,7},{7,6},{8,9},{9,8},{10,11... | collective-permute-start | bytes 786440 | tf_op jit(solution)/shard_map/grads_across/ppermute | solution.py:445
  49.6 4.5 %hidden_units.3 = (f32[512,1024]{1,0:T(8,128)S(1)}, f32[512,1024]{1,0:T(8,128)S(1)}, bf16[512,1024]{1,0:T(8,128)(2,1)S(1)}) custom-call(bf16[128,2176]{1,0:T(8,128)(2,1)S(1)} %collective-permute-done.2.refs_0_.refs_2_, bf16[384,2176]{1,0:T(8,128)(2,1)S(1)} %collective-permute-done.7.refs_1_.refs_3_, ...), custom_call_target="tpu_custom_call" | custom-call | flops 4294967296 | tf_op jit(solution)/shard_map/hidden_units/pallas_call | solution.py:40
  54.1 2.4 %outputs.2 = (bf16[512,1024]{1,0:T(8,128)(2,1)S(1)}, bf16[512,1024]{1,0:T(8,128)(2,1)S(1)}) custom-call(bf16[512,1024]{1,0:T(8,128)(2,1)S(1)} %get-tuple-element.268.gated.refs_5_, bf16[1024,2048]{1,0:T(8,128)(2,1)S(1)} %get-tuple-element.206.down_mat.refs_4_), custom_call_target="tpu_custom_call" | custom-call | tf_op jit(solution)/shard_map/outputs/pallas_call | solution.py:40
  56.6 2.4 %outputs.3 = (bf16[512,1024]{1,0:T(8,128)(2,1)S(1)}, bf16[512,1024]{1,0:T(8,128)(2,1)S(1)}) custom-call(bf16[512,1024]{1,0:T(8,128)(2,1)S(1)} %get-tuple-element.267.gated.refs_4_, bf16[1024,2048]{1,0:T(8,128)(2,1)S(1)} %get-tuple-element.206.down_mat.refs_4_), custom_call_target="tpu_custom_call" | custom-call | tf_op jit(solution)/shard_map/outputs/pallas_call | solution.py:40
  59.4 0.4 collective-permute-start.15
  60.0 3.3 %hidden_grads.2 = (bf16[512,1024]{1,0:T(8,128)(2,1)S(1)}, bf16[512,1024]{1,0:T(8,128)(2,1)S(1)}, bf16[512,128]{1,0:T(8,128)(2,1)S(1)}) custom-call(bf16[128,2048]{1,0:T(8,128)(2,1)S(1)} %get-tuple-element.263.refs_0_, bf16[384,2048]{1,0:T(8,128)(2,1)S(1)} %join.5.refs_1_, bf16[128,2176]{1,0:T(8,128)(2,1)S(1)} %get-tuple-element.291.refs_0_.refs_2_, ...), custom_call_target="tpu_custom_call" | custom-call | tf_op jit(solution)/shard_map/hidden_grads/pallas_call | solution.py:40
  63.4 3.2 %hidden_grads.3 = (bf16[512,1024]{1,0:T(8,128)(2,1)S(1)}, bf16[512,1024]{1,0:T(8,128)(2,1)S(1)}, bf16[512,128]{1,0:T(8,128)(2,1)S(1)}) custom-call(bf16[128,2048]{1,0:T(8,128)(2,1)S(1)} %collective-permute-done.14.refs_0_.refs_2_, bf16[384,2048]{1,0:T(8,128)(2,1)S(1)} %collective-permute-done.15.refs_1_.refs_3_, ...), custom_call_target="tpu_custom_call" | custom-call | tf_op jit(solution)/shard_map/hidden_grads/pallas_call | solution.py:40
  66.5 4.5 %input_grads.2 = (bf16[256,1152]{1,0:T(8,128)(2,1)S(1)}, bf16[256,1152]{1,0:T(8,128)(2,1)S(1)}, bf16[256,1152]{1,0:T(8,128)(2,1)S(1)}, bf16[256,1152]{1,0:T(8,128)(2,1)S(1)}) custom-call(bf16[512,1024]{1,0:T(8,128)(2,1)S(1)} %get-tuple-element.285.d_gate.refs_5_, bf16[512,1024]{1,0:T(8,128)(2,1)S(1)} %get-tuple-element.296.d_up.refs_5_, ...), custom_call_target="tpu_custom_call" | custom-call | tf_op jit(solution)/shard_map/input_grads/pallas_call | solution.py:40
  71.9 4.5 %input_grads.3 = (bf16[512,1152]{1,0:T(8,128)(2,1)S(1)}, bf16[512,1152]{1,0:T(8,128)(2,1)S(1)}) custom-call(bf16[512,1024]{1,0:T(8,128)(2,1)S(1)} %get-tuple-element.284.d_gate.refs_4_, bf16[512,1024]{1,0:T(8,128)(2,1)S(1)} %get-tuple-element.295.d_up.refs_4_, bf16[512,128]{1,0:T(8,128)(2,1)S(1)} %get-tuple-element.250.shares, ...), custom_call_target="tpu_custom_call" | custom-call | tf_op jit(solution)/shard_map/input_grads/pallas_call | solution.py:40
  76.6 3.2 %collective-permute-done.19.arrived = bf16[384,1024]{1,0:T(8,128)(2,1)S(1)} collective-permute-done((bf16[384,1024]{1,0:T(8,128)(2,1)S(1)}, bf16[384,1024]{1,0:T(8,128)(2,1)S(1)}, u32[]{:S(2)}, u32[]{:S(2)}) %collective-permute-start.19) | collective-permute-done | bytes 786464 | tf_op jit(solution)/shard_map/out_across/ppermute | solution.py:445
  80.0 0.4 collective-permute-start.21
  80.5 0.7 collective-permute-start.18
  81.1 6.1 %grad_down.1 = bf16[1024,2048]{1,0:T(8,128)(2,1)} custom-call(bf16[128,2048]{1,0:T(8,128)(2,1)S(1)} %get-tuple-element.263.refs_0_, bf16[384,2048]{1,0:T(8,128)(2,1)S(1)} %join.5.refs_1_, bf16[128,2048]{1,0:T(8,128)(2,1)S(1)} %collective-permute-done.14.refs_0_.refs_2_, bf16[384,2048]{1,0:T(8,128)(2,1)S(1)} %collective-permute-done.15.refs_1_.refs_3_, ...), custom_call_target="tpu_custom_call" | custom-call | flops 4294967296 | tf_op jit(solution)/shard_map/grad_down/pallas_call | solution.py:340
  87.3 2.6 %collective-permute-done.18.arrived = bf16[128,1152]{1,0:T(8,128)(2,1)S(1)} collective-permute-done((bf16[128,1152]{1,0:T(8,128)(2,1)S(1)}, bf16[128,1152]{1,0:T(8,128)(2,1)S(1)}, u32[]{:S(2)}, u32[]{:S(2)}) %collective-permute-start.18) | collective-permute-done | bytes 294944 | tf_op jit(solution)/shard_map/in_across/ppermute | solution.py:445
  90.0 1.7 %collective-permute-start.26 = (bf16[128,1152]{1,0:T(8,128)(2,1)S(1)}, bf16[128,1152]{1,0:T(8,128)(2,1)S(1)}, u32[]{:S(2)}, u32[]{:S(2)}) collective-permute-start(bf16[128,1152]{1,0:T(8,128)(2,1)S(1)} %in_slot.3), channel_id=1, source_target_pairs={{0,4},{2,6},{4,0},{6,2},{8,12},{10,14},{12,8},{14,10},{1,5},{3,7},... | collective-permute-start | bytes 884744 | tf_op jit(solution)/shard_map/in_line/ppermute | solution.py:437
  92.0 1.7 %collective-permute-start.25 = (bf16[128,1152]{1,0:T(8,128)(2,1)S(1)}, bf16[128,1152]{1,0:T(8,128)(2,1)S(1)}, u32[]{:S(2)}, u32[]{:S(2)}) collective-permute-start(bf16[128,1152]{1,0:T(8,128)(2,1)S(1)} %get-tuple-element.279), channel_id=1, source_target_pairs={{0,1},{1,0},{2,3},{3,2},{4,5},{5,4},{6,7},{7,6},{8,9},{9,8},{10,11... | collective-permute-start | bytes 884744 | tf_op jit(solution)/shard_map/in_across/ppermute | solution.py:445
  93.8 0.5 collective-permute-done.21.arrived.near_and_last
  94.4 1.8 %collective-permute-start.23 = (bf16[128,1024]{1,0:T(8,128)(2,1)S(1)}, bf16[128,1024]{1,0:T(8,128)(2,1)S(1)}, u32[]{:S(2)}, u32[]{:S(2)}) collective-permute-start(bf16[128,1024]{1,0:T(8,128)(2,1)S(1)} %add_last.1), channel_id=1, source_target_pairs={{0,8},{2,10},{4,12},{6,14},{8,0},{10,2},{12,4},{14,6},{1,9},{3,11}... | collective-permute-start | bytes 786440 | tf_op jit(solution)/shard_map/out_line/ppermute | solution.py:437
  96.2 6.2 %grad_gate.1 = bf16[2048,1024]{1,0:T(8,128)(2,1)} custom-call(bf16[128,2176]{1,0:T(8,128)(2,1)S(1)} %get-tuple-element.291.refs_0_.refs_2_, bf16[384,2176]{1,0:T(8,128)(2,1)S(1)} %join.4.refs_1_.refs_3_, bf16[128,2176]{1,0:T(8,128)(2,1)S(1)} %collective-permute-done.2.refs_0_.refs_2_, bf16[384,2176]{1,0:T(8,128)(2,1)S(1)} %collective-permute-done.7.refs_1_.refs_3_, ...), custom_call_target="tpu_custom_call" | custom-call | flops 4294967296 | tf_op jit(solution)/shard_map/grad_gate/pallas_call | solution.py:340
  102.4 3.3 %collective-permute-done.25.arrived = bf16[128,1152]{1,0:T(8,128)(2,1)S(1)} collective-permute-done((bf16[128,1152]{1,0:T(8,128)(2,1)S(1)}, bf16[128,1152]{1,0:T(8,128)(2,1)S(1)}, u32[]{:S(2)}, u32[]{:S(2)}) %collective-permute-start.25) | collective-permute-done | bytes 294944 | tf_op jit(solution)/shard_map/in_across/ppermute | solution.py:445
  105.9 2.4 %collective-permute-start.28 = (bf16[128,1152]{1,0:T(8,128)(2,1)S(1)}, bf16[128,1152]{1,0:T(8,128)(2,1)S(1)}, u32[]{:S(2)}, u32[]{:S(2)}) collective-permute-start(bf16[128,1152]{1,0:T(8,128)(2,1)S(1)} %in_slot.4), channel_id=1, source_target_pairs={{0,8},{2,10},{4,12},{6,14},{8,0},{10,2},{12,4},{14,6},{1,9},{3,11}... | collective-permute-start | bytes 884744 | tf_op jit(solution)/shard_map/in_line/ppermute | solution.py:437
  108.2 0.5 collective-permute-start.27
  108.7 6.2 %grad_up.1 = bf16[2048,1024]{1,0:T(8,128)(2,1)} custom-call(bf16[128,2176]{1,0:T(8,128)(2,1)S(1)} %get-tuple-element.291.refs_0_.refs_2_, bf16[384,2176]{1,0:T(8,128)(2,1)S(1)} %join.4.refs_1_.refs_3_, bf16[128,2176]{1,0:T(8,128)(2,1)S(1)} %collective-permute-done.2.refs_0_.refs_2_, bf16[384,2176]{1,0:T(8,128)(2,1)S(1)} %collective-permute-done.7.refs_1_.refs_3_, ...), custom_call_target="tpu_custom_call" | custom-call | flops 4294967296 | tf_op jit(solution)/shard_map/grad_up/pallas_call | solution.py:340
  114.9 0.5 collective-permute-done.27.arrived
  115.5 1.1 collective-permute-start.30
  116.6 1.1 collective-permute-start.29
  117.7 0.9 finish_outputs.1
  118.6 2.1 %collective-permute-done.28.refs_0_ = bf16[128,1152]{1,0:T(8,128)(2,1)S(1)} collective-permute-done((bf16[128,1152]{1,0:T(8,128)(2,1)S(1)}, bf16[128,1152]{1,0:T(8,128)(2,1)S(1)}, u32[]{:S(2)}, u32[]{:S(2)}) %collective-permute-start.28) | collective-permute-done | bytes 294944 | tf_op jit(solution)/shard_map/in_line/ppermute | solution.py:437
  120.7 1.6 %collective-permute-done.30.arrived = bf16[128,1152]{1,0:T(8,128)(2,1)S(1)} collective-permute-done((bf16[128,1152]{1,0:T(8,128)(2,1)S(1)}, bf16[128,1152]{1,0:T(8,128)(2,1)S(1)}, u32[]{:S(2)}, u32[]{:S(2)}) %collective-permute-start.30) | collective-permute-done | bytes 294944 | tf_op jit(solution)/shard_map/in_across/ppermute | solution.py:445
  122.3 4.6 %collective-permute-done.29.refs_1_ = bf16[128,1152]{1,0:T(8,128)(2,1)S(1)} collective-permute-done((bf16[128,1152]{1,0:T(8,128)(2,1)S(1)}, bf16[128,1152]{1,0:T(8,128)(2,1)S(1)}, u32[]{:S(2)}, u32[]{:S(2)}) %collective-permute-start.29) | collective-permute-done | bytes 294944 | tf_op jit(solution)/shard_map/in_line/ppermute | solution.py:437
  126.9 1.1 finish_inputs.1
  (53 shorter events, 3.6 us)
Async XLA Ops:
  1.9 10.5 %collective-permute-start.2 = (bf16[128,2176]{1,0:T(8,128)(2,1)S(1)}, bf16[128,2176]{1,0:T(8,128)(2,1)S(1)}, u32[]{:S(2)}, u32[]{:S(2)}) collective-permute-start(bf16[128,2176]{1,0:T(8,128)(2,1)S(1)} %get-tuple-element.291.refs_0_.refs_2_), channel_id=1, source_target_pairs={{0,2},{2,0},{4,6},{6,4},{8,10},{10,8},{12,14},{14,12},{1,3},{3,1},... | collective-permute-start | bytes 1671176 | tf_op jit(solution)/shard_map/rows_cores/ppermute | solution.py:441
  2.5 17.0 %collective-permute-start.1 = (bf16[64,2176]{1,0:T(8,128)(2,1)S(1)}, bf16[64,2176]{1,0:T(8,128)(2,1)S(1)}, u32[]{:S(2)}, u32[]{:S(2)}) collective-permute-start(bf16[64,2176]{1,0:T(8,128)(2,1)S(1)} %get-tuple-element.162), channel_id=1, source_target_pairs={{0,8},{2,10},{4,12},{6,14},{8,0},{10,2},{12,4},{14,6},{1,9},{3,11}... | collective-permute-start | bytes 835592 | tf_op jit(solution)/shard_map/rows_line/ppermute | solution.py:437
  6.1 13.5 %collective-permute-start = (bf16[64,2176]{1,0:T(8,128)(2,1)S(1)}, bf16[64,2176]{1,0:T(8,128)(2,1)S(1)}, u32[]{:S(2)}, u32[]{:S(2)}) collective-permute-start(bf16[64,2176]{1,0:T(8,128)(2,1)S(1)} %get-tuple-element.162), channel_id=1, source_target_pairs={{0,4},{2,6},{4,0},{6,2},{8,12},{10,14},{12,8},{14,10},{1,5},{3,7},... | collective-permute-start | bytes 835592 | tf_op jit(solution)/shard_map/rows_line/ppermute | solution.py:437
  7.7 15.1 %copy-start = (bf16[128,2048]{1,0:T(8,128)(2,1)S(1)}, bf16[128,2048]{1,0:T(8,128)(2,1)}, u32[]{:S(2)}) copy-start(bf16[128,2048]{1,0:T(8,128)(2,1)} %rows) | copy-start | bytes 1572868
  19.7 12.6 %collective-permute-start.4 = (bf16[64,2176]{1,0:T(8,128)(2,1)S(1)}, bf16[64,2176]{1,0:T(8,128)(2,1)S(1)}, u32[]{:S(2)}, u32[]{:S(2)}) collective-permute-start(bf16[64,2176]{1,0:T(8,128)(2,1)S(1)} %collective-permute-done.1.refs_1_), channel_id=1, source_target_pairs={{0,4},{2,6},{4,0},{6,2},{8,12},{10,14},{12,8},{14,10},{1,5},{3,7},... | collective-permute-start | bytes 835592 | tf_op jit(solution)/shard_map/rows_line/ppermute | solution.py:437
  21.2 21.0 %collective-permute-start.3 = (bf16[128,2176]{1,0:T(8,128)(2,1)S(1)}, bf16[128,2176]{1,0:T(8,128)(2,1)S(1)}, u32[]{:S(2)}, u32[]{:S(2)}) collective-permute-start(bf16[128,2176]{1,0:T(8,128)(2,1)S(1)} %join.3.refs_0_.refs_1_), channel_id=1, source_target_pairs={{0,1},{1,0},{2,3},{3,2},{4,5},{5,4},{6,7},{7,6},{8,9},{9,8},{10,11... | collective-permute-start | bytes 1671176 | tf_op jit(solution)/shard_map/rows_across/ppermute | solution.py:445
  22.8 14.0 %collective-permute-start.6 = (bf16[64,2048]{1,0:T(8,128)(2,1)S(1)}, bf16[64,2048]{1,0:T(8,128)(2,1)S(1)}, u32[]{:S(2)}, u32[]{:S(2)}) collective-permute-start(bf16[64,2048]{1,0:T(8,128)(2,1)S(1)} %get-tuple-element.175), channel_id=1, source_target_pairs={{0,8},{2,10},{4,12},{6,14},{8,0},{10,2},{12,4},{14,6},{1,9},{3,11}... | collective-permute-start | bytes 786440 | tf_op jit(solution)/shard_map/grads_line/ppermute | solution.py:437
  32.3 10.0 %collective-permute-start.5 = (bf16[64,2176]{1,0:T(8,128)(2,1)S(1)}, bf16[64,2176]{1,0:T(8,128)(2,1)S(1)}, u32[]{:S(2)}, u32[]{:S(2)}) collective-permute-start(bf16[64,2176]{1,0:T(8,128)(2,1)S(1)} %collective-permute-done.4.refs_4_), channel_id=1, source_target_pairs={{0,1},{1,0},{2,3},{3,2},{4,5},{5,4},{6,7},{7,6},{8,9},{9,8},{10,11... | collective-permute-start | bytes 835592 | tf_op jit(solution)/shard_map/rows_across/ppermute | solution.py:445
  36.9 10.7 %collective-permute-start.9 = (bf16[64,2048]{1,0:T(8,128)(2,1)S(1)}, bf16[64,2048]{1,0:T(8,128)(2,1)S(1)}, u32[]{:S(2)}, u32[]{:S(2)}) collective-permute-start(bf16[64,2048]{1,0:T(8,128)(2,1)S(1)} %collective-permute-done.6.refs_1_), channel_id=1, source_target_pairs={{0,1},{1,0},{2,3},{3,2},{4,5},{5,4},{6,7},{7,6},{8,9},{9,8},{10,11... | collective-permute-start | bytes 786440 | tf_op jit(solution)/shard_map/grads_across/ppermute | solution.py:445
  37.4 10.2 %collective-permute-start.8 = (bf16[64,2048]{1,0:T(8,128)(2,1)S(1)}, bf16[64,2048]{1,0:T(8,128)(2,1)S(1)}, u32[]{:S(2)}, u32[]{:S(2)}) collective-permute-start(bf16[64,2048]{1,0:T(8,128)(2,1)S(1)} %collective-permute-done.6.refs_1_), channel_id=1, source_target_pairs={{0,4},{2,6},{4,0},{6,2},{8,12},{10,14},{12,8},{14,10},{1,5},{3,7},... | collective-permute-start | bytes 786440 | tf_op jit(solution)/shard_map/grads_line/ppermute | solution.py:437
  37.7 21.3 %collective-permute-start.12 = (bf16[128,2048]{1,0:T(8,128)(2,1)S(1)}, bf16[128,2048]{1,0:T(8,128)(2,1)S(1)}, u32[]{:S(2)}, u32[]{:S(2)}) collective-permute-start(bf16[128,2048]{1,0:T(8,128)(2,1)S(1)} %get-tuple-element.263.refs_0_), channel_id=1, source_target_pairs={{0,4},{2,6},{4,0},{6,2},{8,12},{10,14},{12,8},{14,10},{1,5},{3,7},... | collective-permute-start | bytes 1572872 | tf_op jit(solution)/shard_map/grads_line/ppermute | solution.py:437
  42.4 7.2 %collective-permute-start.7 = (bf16[384,2176]{1,0:T(8,128)(2,1)S(1)}, bf16[384,2176]{1,0:T(8,128)(2,1)S(1)}, u32[]{:S(2)}, u32[]{:S(2)}) collective-permute-start(bf16[384,2176]{1,0:T(8,128)(2,1)S(1)} %join.4.refs_1_.refs_3_), channel_id=1, source_target_pairs={{0,2},{2,0},{4,6},{6,4},{8,10},{10,8},{12,14},{14,12},{1,3},{3,1},... | collective-permute-start | bytes 5013512 | tf_op jit(solution)/shard_map/rows_cores/ppermute | solution.py:441
  47.0 12.0 %collective-permute-start.14 = (bf16[128,2048]{1,0:T(8,128)(2,1)S(1)}, bf16[128,2048]{1,0:T(8,128)(2,1)S(1)}, u32[]{:S(2)}, u32[]{:S(2)}) collective-permute-start(bf16[128,2048]{1,0:T(8,128)(2,1)S(1)} %get-tuple-element.263.refs_0_), channel_id=1, source_target_pairs={{0,2},{2,0},{4,6},{6,4},{8,10},{10,8},{12,14},{14,12},{1,3},{3,1},... | collective-permute-start | bytes 1572872 | tf_op jit(solution)/shard_map/grads_cores/ppermute | solution.py:441
  47.5 11.4 %collective-permute-start.13 = (bf16[64,2048]{1,0:T(8,128)(2,1)S(1)}, bf16[64,2048]{1,0:T(8,128)(2,1)S(1)}, u32[]{:S(2)}, u32[]{:S(2)}) collective-permute-start(bf16[64,2048]{1,0:T(8,128)(2,1)S(1)} %collective-permute-done.8.refs_4_), channel_id=1, source_target_pairs={{0,1},{1,0},{2,3},{3,2},{4,5},{5,4},{6,7},{7,6},{8,9},{9,8},{10,11... | collective-permute-start | bytes 786440 | tf_op jit(solution)/shard_map/grads_across/ppermute | solution.py:445
  56.5 2.7 %collective-permute-start.11 = (bf16[512,1024]{1,0:T(8,128)(2,1)S(1)}, bf16[512,1024]{1,0:T(8,128)(2,1)S(1)}, u32[]{:S(2)}, u32[]{:S(2)}) collective-permute-start(bf16[512,1024]{1,0:T(8,128)(2,1)S(1)} %get-tuple-element.203), channel_id=1, source_target_pairs={{0,2},{2,0},{4,6},{6,4},{8,10},{10,8},{12,14},{14,12},{1,3},{3,1},... | collective-permute-start | bytes 3145736 | tf_op jit(solution)/shard_map/out_cores/ppermute | solution.py:441
  59.4 3.9 %collective-permute-start.15 = (bf16[384,2048]{1,0:T(8,128)(2,1)S(1)}, bf16[384,2048]{1,0:T(8,128)(2,1)S(1)}, u32[]{:S(2)}, u32[]{:S(2)}) collective-permute-start(bf16[384,2048]{1,0:T(8,128)(2,1)S(1)} %join.5.refs_1_), channel_id=1, source_target_pairs={{0,2},{2,0},{4,6},{6,4},{8,10},{10,8},{12,14},{14,12},{1,3},{3,1},... | collective-permute-start | bytes 4718600 | tf_op jit(solution)/shard_map/grads_cores/ppermute | solution.py:441
  59.8 20.0 %collective-permute-start.10 = (bf16[512,1024]{1,0:T(8,128)(2,1)S(1)}, bf16[512,1024]{1,0:T(8,128)(2,1)S(1)}, u32[]{:S(2)}, u32[]{:S(2)}) collective-permute-start(bf16[512,1024]{1,0:T(8,128)(2,1)S(1)} %get-tuple-element.204), channel_id=1, source_target_pairs={{0,2},{2,0},{4,6},{6,4},{8,10},{10,8},{12,14},{14,12},{1,3},{3,1},... | collective-permute-start | bytes 3145736 | tf_op jit(solution)/shard_map/out_cores/ppermute | solution.py:441
  60.0 19.7 %collective-permute-start.19 = (bf16[384,1024]{1,0:T(8,128)(2,1)S(1)}, bf16[384,1024]{1,0:T(8,128)(2,1)S(1)}, u32[]{:S(2)}, u32[]{:S(2)}) collective-permute-start(bf16[384,1024]{1,0:T(8,128)(2,1)S(1)} %get-tuple-element.216), channel_id=1, source_target_pairs={{0,1},{1,0},{2,3},{3,2},{4,5},{5,4},{6,7},{7,6},{8,9},{9,8},{10,11... | collective-permute-start | bytes 2359304 | tf_op jit(solution)/shard_map/out_across/ppermute | solution.py:445
  71.1 5.4 %collective-permute-start.17 = (bf16[256,1152]{1,0:T(8,128)(2,1)S(1)}, bf16[256,1152]{1,0:T(8,128)(2,1)S(1)}, u32[]{:S(2)}, u32[]{:S(2)}) collective-permute-start(bf16[256,1152]{1,0:T(8,128)(2,1)S(1)} %get-tuple-element.245), channel_id=1, source_target_pairs={{0,2},{2,0},{4,6},{6,4},{8,10},{10,8},{12,14},{14,12},{1,3},{3,1},... | collective-permute-start | bytes 1769480 | tf_op jit(solution)/shard_map/in_cores/ppermute | solution.py:441
  71.4 15.8 %collective-permute-start.16 = (bf16[256,1152]{1,0:T(8,128)(2,1)S(1)}, bf16[256,1152]{1,0:T(8,128)(2,1)S(1)}, u32[]{:S(2)}, u32[]{:S(2)}) collective-permute-start(bf16[256,1152]{1,0:T(8,128)(2,1)S(1)} %get-tuple-element.247), channel_id=1, source_target_pairs={{0,2},{2,0},{4,6},{6,4},{8,10},{10,8},{12,14},{14,12},{1,3},{3,1},... | collective-permute-start | bytes 1769480 | tf_op jit(solution)/shard_map/in_cores/ppermute | solution.py:441
  71.6 20.1 %collective-permute-start.22 = (bf16[256,1152]{1,0:T(8,128)(2,1)S(1)}, bf16[256,1152]{1,0:T(8,128)(2,1)S(1)}, u32[]{:S(2)}, u32[]{:S(2)}) collective-permute-start(bf16[256,1152]{1,0:T(8,128)(2,1)S(1)} %get-tuple-element.244), channel_id=1, source_target_pairs={{0,2},{2,0},{4,6},{6,4},{8,10},{10,8},{12,14},{14,12},{1,3},{3,1},... | collective-permute-start | bytes 1769480 | tf_op jit(solution)/shard_map/in_cores/ppermute | solution.py:441
  80.0 14.3 %collective-permute-start.21 = (bf16[256,1024]{1,0:T(8,128)(2,1)S(1)}, bf16[256,1024]{1,0:T(8,128)(2,1)S(1)}, u32[]{:S(2)}, u32[]{:S(2)}) collective-permute-start(bf16[256,1024]{1,0:T(8,128)(2,1)S(1)} %get-tuple-element.261), channel_id=1, source_target_pairs={{0,4},{2,6},{4,0},{6,2},{8,12},{10,14},{12,8},{14,10},{1,5},{3,7},... | collective-permute-start | bytes 1572872 | tf_op jit(solution)/shard_map/out_line/ppermute | solution.py:437
  80.5 34.5 %collective-permute-start.24 = (bf16[256,1152]{1,0:T(8,128)(2,1)S(1)}, bf16[256,1152]{1,0:T(8,128)(2,1)S(1)}, u32[]{:S(2)}, u32[]{:S(2)}) collective-permute-start(bf16[256,1152]{1,0:T(8,128)(2,1)S(1)} %get-tuple-element.246), channel_id=1, source_target_pairs={{0,2},{2,0},{4,6},{6,4},{8,10},{10,8},{12,14},{14,12},{1,3},{3,1},... | collective-permute-start | bytes 1769480 | tf_op jit(solution)/shard_map/in_cores/ppermute | solution.py:441
  80.5 9.4 %collective-permute-start.18 = (bf16[128,1152]{1,0:T(8,128)(2,1)S(1)}, bf16[128,1152]{1,0:T(8,128)(2,1)S(1)}, u32[]{:S(2)}, u32[]{:S(2)}) collective-permute-start(bf16[128,1152]{1,0:T(8,128)(2,1)S(1)} %get-tuple-element.255), channel_id=1, source_target_pairs={{0,1},{1,0},{2,3},{3,2},{4,5},{5,4},{6,7},{7,6},{8,9},{9,8},{10,11... | collective-permute-start | bytes 884744 | tf_op jit(solution)/shard_map/in_across/ppermute | solution.py:445
  90.0 15.7 %collective-permute-start.26 = (bf16[128,1152]{1,0:T(8,128)(2,1)S(1)}, bf16[128,1152]{1,0:T(8,128)(2,1)S(1)}, u32[]{:S(2)}, u32[]{:S(2)}) collective-permute-start(bf16[128,1152]{1,0:T(8,128)(2,1)S(1)} %in_slot.3), channel_id=1, source_target_pairs={{0,4},{2,6},{4,0},{6,2},{8,12},{10,14},{12,8},{14,10},{1,5},{3,7},... | collective-permute-start | bytes 884744 | tf_op jit(solution)/shard_map/in_line/ppermute | solution.py:437
  91.7 10.7 %collective-permute-start.20 = (bf16[128,1024]{1,0:T(8,128)(2,1)S(1)}, bf16[128,1024]{1,0:T(8,128)(2,1)S(1)}, u32[]{:S(2)}, u32[]{:S(2)}) collective-permute-start(bf16[128,1024]{1,0:T(8,128)(2,1)S(1)} %get-tuple-element.272), channel_id=1, source_target_pairs={{0,1},{1,0},{2,3},{3,2},{4,5},{5,4},{6,7},{7,6},{8,9},{9,8},{10,11... | collective-permute-start | bytes 786440 | tf_op jit(solution)/shard_map/out_across/ppermute | solution.py:445
  92.0 13.7 %collective-permute-start.25 = (bf16[128,1152]{1,0:T(8,128)(2,1)S(1)}, bf16[128,1152]{1,0:T(8,128)(2,1)S(1)}, u32[]{:S(2)}, u32[]{:S(2)}) collective-permute-start(bf16[128,1152]{1,0:T(8,128)(2,1)S(1)} %get-tuple-element.279), channel_id=1, source_target_pairs={{0,1},{1,0},{2,3},{3,2},{4,5},{5,4},{6,7},{7,6},{8,9},{9,8},{10,11... | collective-permute-start | bytes 884744 | tf_op jit(solution)/shard_map/in_across/ppermute | solution.py:445
  94.4 23.3 %collective-permute-start.23 = (bf16[128,1024]{1,0:T(8,128)(2,1)S(1)}, bf16[128,1024]{1,0:T(8,128)(2,1)S(1)}, u32[]{:S(2)}, u32[]{:S(2)}) collective-permute-start(bf16[128,1024]{1,0:T(8,128)(2,1)S(1)} %add_last.1), channel_id=1, source_target_pairs={{0,8},{2,10},{4,12},{6,14},{8,0},{10,2},{12,4},{14,6},{1,9},{3,11}... | collective-permute-start | bytes 786440 | tf_op jit(solution)/shard_map/out_line/ppermute | solution.py:437
  105.9 14.8 %collective-permute-start.28 = (bf16[128,1152]{1,0:T(8,128)(2,1)S(1)}, bf16[128,1152]{1,0:T(8,128)(2,1)S(1)}, u32[]{:S(2)}, u32[]{:S(2)}) collective-permute-start(bf16[128,1152]{1,0:T(8,128)(2,1)S(1)} %in_slot.4), channel_id=1, source_target_pairs={{0,8},{2,10},{4,12},{6,14},{8,0},{10,2},{12,4},{14,6},{1,9},{3,11}... | collective-permute-start | bytes 884744 | tf_op jit(solution)/shard_map/in_line/ppermute | solution.py:437
  108.2 7.2 %collective-permute-start.27 = (bf16[128,1152]{1,0:T(8,128)(2,1)S(1)}, bf16[128,1152]{1,0:T(8,128)(2,1)S(1)}, u32[]{:S(2)}, u32[]{:S(2)}) collective-permute-start(bf16[128,1152]{1,0:T(8,128)(2,1)S(1)} %get-tuple-element.290), channel_id=1, source_target_pairs={{0,1},{1,0},{2,3},{3,2},{4,5},{5,4},{6,7},{7,6},{8,9},{9,8},{10,11... | collective-permute-start | bytes 884744 | tf_op jit(solution)/shard_map/in_across/ppermute | solution.py:445
  115.5 6.8 %collective-permute-start.30 = (bf16[128,1152]{1,0:T(8,128)(2,1)S(1)}, bf16[128,1152]{1,0:T(8,128)(2,1)S(1)}, u32[]{:S(2)}, u32[]{:S(2)}) collective-permute-start(bf16[128,1152]{1,0:T(8,128)(2,1)S(1)} %get-tuple-element.306), channel_id=1, source_target_pairs={{0,1},{1,0},{2,3},{3,2},{4,5},{5,4},{6,7},{7,6},{8,9},{9,8},{10,11... | collective-permute-start | bytes 884744 | tf_op jit(solution)/shard_map/in_across/ppermute | solution.py:445
  116.6 10.3 %collective-permute-start.29 = (bf16[128,1152]{1,0:T(8,128)(2,1)S(1)}, bf16[128,1152]{1,0:T(8,128)(2,1)S(1)}, u32[]{:S(2)}, u32[]{:S(2)}) collective-permute-start(bf16[128,1152]{1,0:T(8,128)(2,1)S(1)} %in_slot.5), channel_id=1, source_target_pairs={{0,4},{2,6},{4,0},{6,2},{8,12},{10,14},{12,8},{14,10},{1,5},{3,7},... | collective-permute-start | bytes 884744 | tf_op jit(solution)/shard_map/in_line/ppermute | solution.py:437
  118.6 8.3 %copy-start.1 = (s32[128,4]{0,1:T(4,128)S(1)}, s32[128,4]{0,1:T(4,128)}, u32[]{:S(2)}) copy-start(s32[128,4]{0,1:T(4,128)} %param.9) | copy-start | bytes 6148
  118.6 8.3 %copy-start.2 = (f32[128,4]{0,1:T(4,128)S(1)}, f32[128,4]{0,1:T(4,128)}, u32[]{:S(2)}) copy-start(f32[128,4]{0,1:T(4,128)} %param.11) | copy-start | bytes 6148
  118.6 8.3 %copy-start.3 = (s32[128]{0:T(128)S(1)}, s32[128]{0:T(128)}, u32[]{:S(2)}) copy-start(s32[128]{0:T(128)} %param.10) | copy-start | bytes 1540
where the time goes:
time: 128 us
  Pallas kernels  57 us (45%)
  waiting for transfers between devices  37.9 us (30%)
  starting transfers between devices  32.1 us (25%)
    pallas_call x22, Pallas kernels, call(): pl.pallas_call(kernel, out_shape=out_shape, in_specs=[VMEM] * len(operand...  32.6 us
    ppermute x11, waiting for transfers between devices, line(): return lax.ppermute(array, 'expert', pairs)  23.7 us
    ppermute x11, starting transfers between devices, line(): return lax.ppermute(array, 'expert', pairs)  18.6 us
    pallas_call x3, Pallas kernels, weights(): pl.pallas_call(functools.partial(weights_kernel, width, 512), out_shape=j...  18.5 us
    ppermute x10, waiting for transfers between devices, across(): return lax.ppermute(array, 'helper', self.sides)  14 us
    ppermute x10, starting transfers between devices, across(): return lax.ppermute(array, 'helper', self.sides)  10.8 us
    pallas_call x1, Pallas kernels, load(): pl.pallas_call(load_kernel, out_shape=tuple((jax.ShapeDtypeStruct(mat.sha...  4.73 us
    ppermute x10, starting transfers between devices, sibling(): return lax.ppermute(array, 'expert', self.cores)  2.64 us
  transfers between devices with their start and end apart: 31, of which 14 were waited for; matrix products, arithmetic and copies ran while one was open for 0% of the time, Pallas kernels for 43%

commit v1 on v0

--- a/solution.py
+++ b/solution.py
@@ -333,7 +333,7 @@
         copy(step).wait()
 
 
-def weights(name, pieces, acts, width, by_hidden):
+def weights(name, pieces, acts, width, by_hidden, flops=0):
     rows, hidden = acts[0].shape
     shape = (hidden, width) if by_hidden else (width, hidden)
     operands = (*pieces, *acts)
@@ -350,7 +350,7 @@
         ],
         compiler_params=pltpu.CompilerParams(vmem_limit_bytes=16 * 2**20),
         cost_estimate=pl.CostEstimate(
-            flops=4 * rows * width * hidden, bytes_accessed=0, transcendentals=0
+            flops=flops, bytes_accessed=0, transcendentals=0
         ),
         name=name,
     )(*operands)
@@ -388,8 +388,8 @@
     total[...] = far_slot[...] + arrived[rows:, :]
 
 
-def slot_kernel(slot, own, received, arrived, *refs):
-    whole = slot_sum(own, received, arrived, slot, 0, slot % 2)
+def slot_kernel(slot, offset, own, received, arrived, *refs):
+    whole = slot_sum(own, received, arrived, slot, offset, slot % 2)
     if len(refs) > 1:
         whole = whole + refs[0][...].astype(jnp.float32)
     refs[-1][...] = whole.astype(refs[-1].dtype)
@@ -463,12 +463,12 @@
             (shape(2), shape(1)),
         )
 
-    def slot(self, which, own, received, arrived, *others):
+    def slot(self, which, offset, own, received, arrived, *others):
         return call(
-            functools.partial(slot_kernel, which),
+            functools.partial(slot_kernel, which, offset),
             self.label + "_slot",
             (own, received, arrived, *others),
-            jax.ShapeDtypeStruct(arrived.shape, arrived.dtype),
+            jax.ShapeDtypeStruct((own.shape[0] // 4, own.shape[1]), own.dtype),
         )
 
 
@@ -528,7 +528,10 @@
     rows, grads, outs, ins = (FourChips(label) for label in ("rows", "grads", "out", "in"))
     order = Order()
     hold = lambda value, *tokens: lax.optimization_barrier((value, tokens))[0]
-    product_of = lambda name, by_hidden: lambda r, acts: weights(name, r, acts, width, by_hidden)
+    product_of = lambda name, by_hidden, flops=0: lambda r, acts: weights(
+        name, r, acts, width, by_hidden, flops
+    )
+    estimate = 16 * tokens.size * gate_local.shape[1]
 
     size = tokens.shape[0]
     half = size // 2
@@ -603,34 +606,33 @@
     in_send, in_keep = order(
         lambda *d: input_grads_of(1, *d, gate_mat, up_mat), own_d_gate, own_d_up, own_shares
     )
-    far_sent, last_sent = order(
-        lambda *s: ins.send(2 * size, *s, (size, size)), in_send, far_received
-    )
-    last_arrived = ins.across(last_sent)
-    near_slots, far_slot = order(outs.slots, out_keep, kept, hold(arrived, far_sent))
+    (sent,) = order(lambda *s: ins.send(2 * size, *s, (2 * size,)), in_send, far_received)
+    far_arrived = ins.across(sent)
+    near_slots, far_slot = order(outs.slots, out_keep, kept, hold(arrived, sent))
     near_sums = outs.line(near_slots, outs.near)
-    grad_down = order(product_of("grad_down", True), own_grads + other_grads, (own_act, other_act))
-    slot = order(lambda *s: ins.slot(3, *s), in_keep, far_kept, last_arrived)
-    last_sum = ins.line(slot, ins.near)
-    far_arrived = ins.across(hold(far_sent, slot))
-    out_arrived = outs.across(hold(out_sent, slot))
-    own_sent, near_sent = order(
-        lambda *s: ins.send(0, *s, (size, size)), in_send, near_received
-    )
+    grad_down = order(product_of("grad_down", True, estimate), own_grads + other_grads, (own_act, other_act))
     far_slot = order(
         lambda *s: call(add_last_kernel, "add_last", s, jax.ShapeDtypeStruct(s[0].shape, s[0].dtype)),
         far_slot,
         near_sums,
     )
     far_sum = outs.line(far_slot, outs.far)
-    grad_gate = order(product_of("grad_gate", False), own_rows + other_rows, (own_d_gate, other_d_gate))
+    slot = order(lambda *s: ins.slot(3, size, *s), in_keep, far_kept, far_arrived)
+    last_sum = ins.line(slot, ins.near)
+    own_sent, near_sent = order(
+        lambda *s: ins.send(0, *s, (size, size)), in_send, near_received
+    )
+    near_arrived = ins.across(near_sent)
+    out_arrived = outs.across(hold(out_sent, slot))
+    grad_gate = order(
+        product_of("grad_gate", False, estimate), own_rows + other_rows, (own_d_gate, other_d_gate)
+    )
+    slot = order(lambda *s: ins.slot(2, 0, *s), in_keep, far_kept, far_arrived, last_sum)
+    far = ins.line(slot, ins.far)
+    near_arrived = hold(near_arrived, slot)
     slot = order(
-        lambda *s: ins.slot(2, *s), in_keep, far_kept, far_arrived, last_sum, also=out_arrived
-    )
-    far = ins.line(slot, ins.far)
-    near_arrived = ins.across(hold(near_sent, slot))
-    grad_up = order(product_of("grad_up", False), own_rows + other_rows, (own_d_up, other_d_up))
-    slot = order(lambda *s: ins.slot(1, *s), in_keep, near_kept, near_arrived)
+        lambda *s: ins.slot(1, 0, *s), in_keep, near_kept, near_arrived, also=out_arrived
+    )
     near = ins.line(slot, ins.near)
     own_arrived = ins.across(hold(own_sent, slot))
     columns = jax.ShapeDtypeStruct((size, width // 2), jnp.bfloat16)
@@ -641,6 +643,10 @@
         out_arrived,
         near_sums,
         far_sum,
+    )
+    clock = order(lambda c: space(c, 10**9), clock)
+    grad_up = order(
+        product_of("grad_up", False), own_rows + other_rows, (own_d_up, other_d_up)
     )
     clock = order(lambda c: space(c, 2 * 10**9), clock, also=far)
     near, own_arrived = hold((near, own_arrived), clock)

time: 128 us -> 123 us (0.961)
  starting transfers between devices: 32.1 us -> 28.6 us
  waiting for transfers between devices: 37.9 us -> 35.7 us
    ppermute x10 -> x9, waiting for transfers between devices: 14 us -> 4.68 us  [across(): return lax.ppermute(array, 'helper', self.sides)]
    ppermute x11, waiting for transfers between devices: 23.7 us -> 30.8 us  [line(): return lax.ppermute(array, 'expert', pairs)]
    ppermute x11, starting transfers between devices: 18.6 us -> 15 us  [line(): return lax.ppermute(array, 'expert', pairs)]
    ppermute x10 -> x9, starting transfers between devices: 10.8 us -> 11.1 us  [across(): return lax.ppermute(array, 'helper', self.sides)]
  transfers between devices with their start and end apart: 31 -> 30, of which waited for: 14 -> 11; matrix products, arithmetic and copies ran while one was open for 0% -> 0% of each run, Pallas kernels for 43% -> 45%
where the time goes in v1:
time: 123 us; the launch traced here: 122 us
  Pallas kernels  57.1 us (46%)
  waiting for transfers between devices  35.7 us (29%)
  starting transfers between devices  28.6 us (23%)
    pallas_call x22, Pallas kernels, call(): pl.pallas_call(kernel, out_shape=out_shape, in_specs=[VMEM] * len(operand...  32.6 us
    ppermute x11, waiting for transfers between devices, line(): return lax.ppermute(array, 'expert', pairs)  30.8 us
    pallas_call x3, Pallas kernels, weights(): pl.pallas_call(functools.partial(weights_kernel, width, 512), out_shape=j...  18.5 us
    ppermute x11, starting transfers between devices, line(): return lax.ppermute(array, 'expert', pairs)  15 us
    ppermute x9, starting transfers between devices, across(): return lax.ppermute(array, 'helper', self.sides)  11.1 us
    pallas_call x1, Pallas kernels, load(): pl.pallas_call(load_kernel, out_shape=tuple((jax.ShapeDtypeStruct(mat.sha...  4.73 us
    ppermute x9, waiting for transfers between devices, across(): return lax.ppermute(array, 'helper', self.sides)  4.68 us
  transfers between devices with their start and end apart: 30, of which 11 were waited for; matrix products, arithmetic and copies ran while one was open for 0% of the time, Pallas kernels for 45%

profile of v1, /device:TPU:0, one launch (start us, length us, event | category | flops | bytes accessed | tf_op | source)
XLA Modules:
  0.0 122.3 jit_solution(16618997035683300895)
XLA Ops:
  0.6 1.3 %prepare_rows.1 = (bf16[64,2176]{1,0:T(8,128)(2,1)S(1)}, bf16[128,2176]{1,0:T(8,128)(2,1)S(1)}, f32[8,128]{1,0:T(8,128)S(1)}) custom-call(s32[4,128]{1,0:T(4,128)} %bitcast.10, s32[1,128]{1,0:T(1,128)} %bitcast.14, f32[4,128]{1,0:T(4,128)} %bitcast.12, bf16[128,2048]{1,0:T(8,128)(2,1)} %refs_3_.1), custom_call_target="tpu_custom_call" | custom-call | tf_op jit(solution)/shard_map/prepare_rows/pallas_call | solution.py:112
  1.9 0.5 collective-permute-start.2
  2.5 3.7 %collective-permute-start.1 = (bf16[64,2176]{1,0:T(8,128)(2,1)S(1)}, bf16[64,2176]{1,0:T(8,128)(2,1)S(1)}, u32[]{:S(2)}, u32[]{:S(2)}) collective-permute-start(bf16[64,2176]{1,0:T(8,128)(2,1)S(1)} %get-tuple-element.160), channel_id=1, source_target_pairs={{0,8},{2,10},{4,12},{6,14},{8,0},{10,2},{12,4},{14,6},{1,9},{3,11}... | collective-permute-start | bytes 835592 | tf_op jit(solution)/shard_map/rows_line/ppermute | solution.py:437
  6.1 1.6 %collective-permute-start = (bf16[64,2176]{1,0:T(8,128)(2,1)S(1)}, bf16[64,2176]{1,0:T(8,128)(2,1)S(1)}, u32[]{:S(2)}, u32[]{:S(2)}) collective-permute-start(bf16[64,2176]{1,0:T(8,128)(2,1)S(1)} %get-tuple-element.160), channel_id=1, source_target_pairs={{0,4},{2,6},{4,0},{6,2},{8,12},{10,14},{12,8},{14,10},{1,5},{3,7},... | collective-permute-start | bytes 835592 | tf_op jit(solution)/shard_map/rows_line/ppermute | solution.py:437
  7.7 4.7 %load.1 = (bf16[2048,1024]{1,0:T(8,128)(2,1)S(1)}, bf16[2048,1024]{1,0:T(8,128)(2,1)S(1)}, bf16[1024,2048]{1,0:T(8,128)(2,1)S(1)}) custom-call(bf16[2048,1024]{1,0:T(8,128)(2,1)} %bitcast.16, bf16[2048,1024]{1,0:T(8,128)(2,1)} %bitcast.17, bf16[1024,2048]{1,0:T(8,128)(2,1)} %bitcast.18), custom_call_target="tpu_custom_call" | custom-call | tf_op jit(solution)/shard_map/load/pallas_call | solution.py:488
  12.4 7.0 %collective-permute-done.1.refs_1_ = bf16[64,2176]{1,0:T(8,128)(2,1)S(1)} collective-permute-done((bf16[64,2176]{1,0:T(8,128)(2,1)S(1)}, bf16[64,2176]{1,0:T(8,128)(2,1)S(1)}, u32[]{:S(2)}, u32[]{:S(2)}) %collective-permute-start.1) | collective-permute-done | bytes 278560 | tf_op jit(solution)/shard_map/rows_line/ppermute | solution.py:437
  19.7 1.6 %collective-permute-start.4 = (bf16[64,2176]{1,0:T(8,128)(2,1)S(1)}, bf16[64,2176]{1,0:T(8,128)(2,1)S(1)}, u32[]{:S(2)}, u32[]{:S(2)}) collective-permute-start(bf16[64,2176]{1,0:T(8,128)(2,1)S(1)} %collective-permute-done.1.refs_1_), channel_id=1, source_target_pairs={{0,4},{2,6},{4,0},{6,2},{8,12},{10,14},{12,8},{14,10},{1,5},{3,7},... | collective-permute-start | bytes 835592 | tf_op jit(solution)/shard_map/rows_line/ppermute | solution.py:437
  21.2 1.5 %collective-permute-start.3 = (bf16[128,2176]{1,0:T(8,128)(2,1)S(1)}, bf16[128,2176]{1,0:T(8,128)(2,1)S(1)}, u32[]{:S(2)}, u32[]{:S(2)}) collective-permute-start(bf16[128,2176]{1,0:T(8,128)(2,1)S(1)} %join.3.refs_0_.refs_1_), channel_id=1, source_target_pairs={{0,1},{1,0},{2,3},{3,2},{4,5},{5,4},{6,7},{7,6},{8,9},{9,8},{10,11... | collective-permute-start | bytes 1671176 | tf_op jit(solution)/shard_map/rows_across/ppermute | solution.py:445
  22.8 2.4 %collective-permute-start.6 = (bf16[64,2048]{1,0:T(8,128)(2,1)S(1)}, bf16[64,2048]{1,0:T(8,128)(2,1)S(1)}, u32[]{:S(2)}, u32[]{:S(2)}) collective-permute-start(bf16[64,2048]{1,0:T(8,128)(2,1)S(1)} %get-tuple-element.173), channel_id=1, source_target_pairs={{0,8},{2,10},{4,12},{6,14},{8,0},{10,2},{12,4},{14,6},{1,9},{3,11}... | collective-permute-start | bytes 786440 | tf_op jit(solution)/shard_map/grads_line/ppermute | solution.py:437
  25.2 7.1 %collective-permute-done.4.refs_4_ = bf16[64,2176]{1,0:T(8,128)(2,1)S(1)} collective-permute-done((bf16[64,2176]{1,0:T(8,128)(2,1)S(1)}, bf16[64,2176]{1,0:T(8,128)(2,1)S(1)}, u32[]{:S(2)}, u32[]{:S(2)}) %collective-permute-start.4) | collective-permute-done | bytes 278560 | tf_op jit(solution)/shard_map/rows_line/ppermute | solution.py:437
  32.3 2.4 %collective-permute-start.5 = (bf16[64,2176]{1,0:T(8,128)(2,1)S(1)}, bf16[64,2176]{1,0:T(8,128)(2,1)S(1)}, u32[]{:S(2)}, u32[]{:S(2)}) collective-permute-start(bf16[64,2176]{1,0:T(8,128)(2,1)S(1)} %collective-permute-done.4.refs_4_), channel_id=1, source_target_pairs={{0,1},{1,0},{2,3},{3,2},{4,5},{5,4},{6,7},{7,6},{8,9},{9,8},{10,11... | collective-permute-start | bytes 835592 | tf_op jit(solution)/shard_map/rows_across/ppermute | solution.py:445
  34.7 2.2 %collective-permute-done.6.refs_1_ = bf16[64,2048]{1,0:T(8,128)(2,1)S(1)} collective-permute-done((bf16[64,2048]{1,0:T(8,128)(2,1)S(1)}, bf16[64,2048]{1,0:T(8,128)(2,1)S(1)}, u32[]{:S(2)}, u32[]{:S(2)}) %collective-permute-start.6) | collective-permute-done | bytes 262176 | tf_op jit(solution)/shard_map/grads_line/ppermute | solution.py:437
  36.9 0.5 collective-permute-start.9
  37.4 0.3 collective-permute-start.8
  37.7 1.7 %collective-permute-start.12 = (bf16[128,2048]{1,0:T(8,128)(2,1)S(1)}, bf16[128,2048]{1,0:T(8,128)(2,1)S(1)}, u32[]{:S(2)}, u32[]{:S(2)}) collective-permute-start(bf16[128,2048]{1,0:T(8,128)(2,1)S(1)} %get-tuple-element.259.refs_0_), channel_id=1, source_target_pairs={{0,4},{2,6},{4,0},{6,2},{8,12},{10,14},{12,8},{14,10},{1,5},{3,7},... | collective-permute-start | bytes 1572872 | tf_op jit(solution)/shard_map/grads_line/ppermute | solution.py:437
  39.4 2.9 %collective-permute-done.5.refs_5_ = bf16[64,2176]{1,0:T(8,128)(2,1)S(1)} collective-permute-done((bf16[64,2176]{1,0:T(8,128)(2,1)S(1)}, bf16[64,2176]{1,0:T(8,128)(2,1)S(1)}, u32[]{:S(2)}, u32[]{:S(2)}) %collective-permute-start.5) | collective-permute-done | bytes 278560 | tf_op jit(solution)/shard_map/rows_across/ppermute | solution.py:445
  42.5 4.5 %hidden_units.2 = (f32[512,1024]{1,0:T(8,128)S(1)}, f32[512,1024]{1,0:T(8,128)S(1)}, bf16[512,1024]{1,0:T(8,128)(2,1)S(1)}) custom-call(bf16[128,2176]{1,0:T(8,128)(2,1)S(1)} %get-tuple-element.295.refs_0_.refs_2_, bf16[384,2176]{1,0:T(8,128)(2,1)S(1)} %join.4.refs_1_.refs_3_, bf16[2048,1024]{1,0:T(8,128)(2,1)S(1)} %get-tuple-element.165.refs_2_.gate_mat, ...), custom_call_target="tpu_custom_call" | custom-call | flops 4294967296 | tf_op jit(solution)/shard_map/hidden_units/pallas_call | solution.py:40
  47.0 0.5 collective-permute-start.14
  47.5 2.0 %collective-permute-start.13 = (bf16[64,2048]{1,0:T(8,128)(2,1)S(1)}, bf16[64,2048]{1,0:T(8,128)(2,1)S(1)}, u32[]{:S(2)}, u32[]{:S(2)}) collective-permute-start(bf16[64,2048]{1,0:T(8,128)(2,1)S(1)} %collective-permute-done.8.refs_4_), channel_id=1, source_target_pairs={{0,1},{1,0},{2,3},{3,2},{4,5},{5,4},{6,7},{7,6},{8,9},{9,8},{10,11... | collective-permute-start | bytes 786440 | tf_op jit(solution)/shard_map/grads_across/ppermute | solution.py:445
  49.6 4.5 %hidden_units.3 = (f32[512,1024]{1,0:T(8,128)S(1)}, f32[512,1024]{1,0:T(8,128)S(1)}, bf16[512,1024]{1,0:T(8,128)(2,1)S(1)}) custom-call(bf16[128,2176]{1,0:T(8,128)(2,1)S(1)} %collective-permute-done.2.refs_0_.refs_2_, bf16[384,2176]{1,0:T(8,128)(2,1)S(1)} %collective-permute-done.7.refs_1_.refs_3_, ...), custom_call_target="tpu_custom_call" | custom-call | flops 4294967296 | tf_op jit(solution)/shard_map/hidden_units/pallas_call | solution.py:40
  54.1 2.4 %outputs.2 = (bf16[512,1024]{1,0:T(8,128)(2,1)S(1)}, bf16[512,1024]{1,0:T(8,128)(2,1)S(1)}) custom-call(bf16[512,1024]{1,0:T(8,128)(2,1)S(1)} %get-tuple-element.264.gated.refs_5_, bf16[1024,2048]{1,0:T(8,128)(2,1)S(1)} %get-tuple-element.204.down_mat.refs_4_), custom_call_target="tpu_custom_call" | custom-call | tf_op jit(solution)/shard_map/outputs/pallas_call | solution.py:40
  56.6 2.4 %outputs.3 = (bf16[512,1024]{1,0:T(8,128)(2,1)S(1)}, bf16[512,1024]{1,0:T(8,128)(2,1)S(1)}) custom-call(bf16[512,1024]{1,0:T(8,128)(2,1)S(1)} %get-tuple-element.263.gated.refs_4_, bf16[1024,2048]{1,0:T(8,128)(2,1)S(1)} %get-tuple-element.204.down_mat.refs_4_), custom_call_target="tpu_custom_call" | custom-call | tf_op jit(solution)/shard_map/outputs/pallas_call | solution.py:40
  59.0 0.2 collective-permute-done.11.received
  59.4 0.4 collective-permute-start.15
  59.8 0.2 collective-permute-start.10
  60.0 3.3 %hidden_grads.2 = (bf16[512,1024]{1,0:T(8,128)(2,1)S(1)}, bf16[512,1024]{1,0:T(8,128)(2,1)S(1)}, bf16[512,128]{1,0:T(8,128)(2,1)S(1)}) custom-call(bf16[128,2048]{1,0:T(8,128)(2,1)S(1)} %get-tuple-element.259.refs_0_, bf16[384,2048]{1,0:T(8,128)(2,1)S(1)} %join.5.refs_1_, bf16[128,2176]{1,0:T(8,128)(2,1)S(1)} %get-tuple-element.295.refs_0_.refs_2_, ...), custom_call_target="tpu_custom_call" | custom-call | tf_op jit(solution)/shard_map/hidden_grads/pallas_call | solution.py:40
  63.4 3.2 %hidden_grads.3 = (bf16[512,1024]{1,0:T(8,128)(2,1)S(1)}, bf16[512,1024]{1,0:T(8,128)(2,1)S(1)}, bf16[512,128]{1,0:T(8,128)(2,1)S(1)}) custom-call(bf16[128,2048]{1,0:T(8,128)(2,1)S(1)} %collective-permute-done.14.refs_0_.refs_2_, bf16[384,2048]{1,0:T(8,128)(2,1)S(1)} %collective-permute-done.15.refs_1_.refs_3_, ...), custom_call_target="tpu_custom_call" | custom-call | tf_op jit(solution)/shard_map/hidden_grads/pallas_call | solution.py:40
  66.5 4.5 %input_grads.2 = (bf16[256,1152]{1,0:T(8,128)(2,1)S(1)}, bf16[256,1152]{1,0:T(8,128)(2,1)S(1)}, bf16[256,1152]{1,0:T(8,128)(2,1)S(1)}, bf16[256,1152]{1,0:T(8,128)(2,1)S(1)}) custom-call(bf16[512,1024]{1,0:T(8,128)(2,1)S(1)} %get-tuple-element.280.d_gate.refs_5_, bf16[512,1024]{1,0:T(8,128)(2,1)S(1)} %get-tuple-element.300.d_up.refs_5_, ...), custom_call_target="tpu_custom_call" | custom-call | tf_op jit(solution)/shard_map/input_grads/pallas_call | solution.py:40
  71.1 0.3 collective-permute-start.17
  71.4 0.2 collective-permute-start.16
  71.6 4.5 %input_grads.3 = (bf16[512,1152]{1,0:T(8,128)(2,1)S(1)}, bf16[512,1152]{1,0:T(8,128)(2,1)S(1)}) custom-call(bf16[512,1024]{1,0:T(8,128)(2,1)S(1)} %get-tuple-element.279.d_gate.refs_4_, bf16[512,1024]{1,0:T(8,128)(2,1)S(1)} %get-tuple-element.299.d_up.refs_4_, bf16[512,128]{1,0:T(8,128)(2,1)S(1)} %get-tuple-element.248.shares, ...), custom_call_target="tpu_custom_call" | custom-call | tf_op jit(solution)/shard_map/input_grads/pallas_call | solution.py:40
  76.3 2.1 %collective-permute-start.18 = (bf16[256,1152]{1,0:T(8,128)(2,1)S(1)}, bf16[256,1152]{1,0:T(8,128)(2,1)S(1)}, u32[]{:S(2)}, u32[]{:S(2)}) collective-permute-start(bf16[256,1152]{1,0:T(8,128)(2,1)S(1)} %in_send.2), channel_id=1, source_target_pairs={{0,1},{1,0},{2,3},{3,2},{4,5},{5,4},{6,7},{7,6},{8,9},{9,8},{10,11... | collective-permute-start | bytes 1769480 | tf_op jit(solution)/shard_map/in_across/ppermute | solution.py:445
  78.3 1.8 %collective-permute-done.19.arrived = bf16[384,1024]{1,0:T(8,128)(2,1)S(1)} collective-permute-done((bf16[384,1024]{1,0:T(8,128)(2,1)S(1)}, bf16[384,1024]{1,0:T(8,128)(2,1)S(1)}, u32[]{:S(2)}, u32[]{:S(2)}) %collective-permute-start.19) | collective-permute-done | bytes 786464 | tf_op jit(solution)/shard_map/out_across/ppermute | solution.py:445
  80.1 0.3 out_slots.1
  80.6 6.1 %grad_down.1 = bf16[1024,2048]{1,0:T(8,128)(2,1)} custom-call(bf16[128,2048]{1,0:T(8,128)(2,1)S(1)} %get-tuple-element.259.refs_0_, bf16[384,2048]{1,0:T(8,128)(2,1)S(1)} %join.5.refs_1_, bf16[128,2048]{1,0:T(8,128)(2,1)S(1)} %collective-permute-done.14.refs_0_.refs_2_, bf16[384,2048]{1,0:T(8,128)(2,1)S(1)} %collective-permute-done.15.refs_1_.refs_3_, ...), custom_call_target="tpu_custom_call" | custom-call | flops 4294967296 | tf_op jit(solution)/shard_map/grad_down/pallas_call | solution.py:340
  86.7 6.7 %collective-permute-done.20.arrived.near_and_last = bf16[256,1024]{1,0:T(8,128)(2,1)S(1)} collective-permute-done((bf16[256,1024]{1,0:T(8,128)(2,1)S(1)}, bf16[256,1024]{1,0:T(8,128)(2,1)S(1)}, u32[]{:S(2)}, u32[]{:S(2)}) %collective-permute-start.20) | collective-permute-done | bytes 524320 | tf_op jit(solution)/shard_map/out_line/ppermute | solution.py:437
  93.4 2.4 %collective-permute-start.22 = (bf16[128,1024]{1,0:T(8,128)(2,1)S(1)}, bf16[128,1024]{1,0:T(8,128)(2,1)S(1)}, u32[]{:S(2)}, u32[]{:S(2)}) collective-permute-start(bf16[128,1024]{1,0:T(8,128)(2,1)S(1)} %add_last.1), channel_id=1, source_target_pairs={{0,8},{2,10},{4,12},{6,14},{8,0},{10,2},{12,4},{14,6},{1,9},{3,11}... | collective-permute-start | bytes 786440 | tf_op jit(solution)/shard_map/out_line/ppermute | solution.py:437
  95.9 1.1 collective-permute-start.26
  97.1 0.7 collective-permute-start.25
  97.8 1.4 %collective-permute-start.21 = (bf16[128,1024]{1,0:T(8,128)(2,1)S(1)}, bf16[128,1024]{1,0:T(8,128)(2,1)S(1)}, u32[]{:S(2)}, u32[]{:S(2)}) collective-permute-start(bf16[128,1024]{1,0:T(8,128)(2,1)S(1)} %get-tuple-element.270), channel_id=1, source_target_pairs={{0,1},{1,0},{2,3},{3,2},{4,5},{5,4},{6,7},{7,6},{8,9},{9,8},{10,11... | collective-permute-start | bytes 786440 | tf_op jit(solution)/shard_map/out_across/ppermute | solution.py:445
  99.2 6.2 %grad_gate.1 = bf16[2048,1024]{1,0:T(8,128)(2,1)} custom-call(bf16[128,2176]{1,0:T(8,128)(2,1)S(1)} %get-tuple-element.295.refs_0_.refs_2_, bf16[384,2176]{1,0:T(8,128)(2,1)S(1)} %join.4.refs_1_.refs_3_, bf16[128,2176]{1,0:T(8,128)(2,1)S(1)} %collective-permute-done.2.refs_0_.refs_2_, bf16[384,2176]{1,0:T(8,128)(2,1)S(1)} %collective-permute-done.7.refs_1_.refs_3_, ...), custom_call_target="tpu_custom_call" | custom-call | flops 4294967296 | tf_op jit(solution)/shard_map/grad_gate/pallas_call | solution.py:340
  105.4 4.9 %collective-permute-done.26.refs_0_ = bf16[128,1152]{1,0:T(8,128)(2,1)S(1)} collective-permute-done((bf16[128,1152]{1,0:T(8,128)(2,1)S(1)}, bf16[128,1152]{1,0:T(8,128)(2,1)S(1)}, u32[]{:S(2)}, u32[]{:S(2)}) %collective-permute-start.26) | collective-permute-done | bytes 294944 | tf_op jit(solution)/shard_map/in_line/ppermute | solution.py:437
  110.7 0.5 collective-permute-start.29
  111.5 0.9 finish_outputs.1
  112.3 6.2 %grad_up.1 = bf16[2048,1024]{1,0:T(8,128)(2,1)} custom-call(bf16[128,2176]{1,0:T(8,128)(2,1)S(1)} %get-tuple-element.295.refs_0_.refs_2_, bf16[384,2176]{1,0:T(8,128)(2,1)S(1)} %join.4.refs_1_.refs_3_, bf16[128,2176]{1,0:T(8,128)(2,1)S(1)} %collective-permute-done.2.refs_0_.refs_2_, bf16[384,2176]{1,0:T(8,128)(2,1)S(1)} %collective-permute-done.7.refs_1_.refs_3_, ...), custom_call_target="tpu_custom_call" | custom-call | tf_op jit(solution)/shard_map/grad_up/pallas_call | solution.py:340
  118.6 2.4 %collective-permute-done.27.refs_0_ = bf16[128,1152]{1,0:T(8,128)(2,1)S(1)} collective-permute-done((bf16[128,1152]{1,0:T(8,128)(2,1)S(1)}, bf16[128,1152]{1,0:T(8,128)(2,1)S(1)}, u32[]{:S(2)}, u32[]{:S(2)}) %collective-permute-start.27) | collective-permute-done | bytes 294944 | tf_op jit(solution)/shard_map/in_line/ppermute | solution.py:437
  121.0 0.3 collective-permute-done.28.refs_1_
  121.3 1.1 finish_inputs.1
  (52 shorter events, 1.8 us)
Async XLA Ops:
  1.9 10.5 %collective-permute-start.2 = (bf16[128,2176]{1,0:T(8,128)(2,1)S(1)}, bf16[128,2176]{1,0:T(8,128)(2,1)S(1)}, u32[]{:S(2)}, u32[]{:S(2)}) collective-permute-start(bf16[128,2176]{1,0:T(8,128)(2,1)S(1)} %get-tuple-element.295.refs_0_.refs_2_), channel_id=1, source_target_pairs={{0,2},{2,0},{4,6},{6,4},{8,10},{10,8},{12,14},{14,12},{1,3},{3,1},... | collective-permute-start | bytes 1671176 | tf_op jit(solution)/shard_map/rows_cores/ppermute | solution.py:441
  2.5 17.0 %collective-permute-start.1 = (bf16[64,2176]{1,0:T(8,128)(2,1)S(1)}, bf16[64,2176]{1,0:T(8,128)(2,1)S(1)}, u32[]{:S(2)}, u32[]{:S(2)}) collective-permute-start(bf16[64,2176]{1,0:T(8,128)(2,1)S(1)} %get-tuple-element.160), channel_id=1, source_target_pairs={{0,8},{2,10},{4,12},{6,14},{8,0},{10,2},{12,4},{14,6},{1,9},{3,11}... | collective-permute-start | bytes 835592 | tf_op jit(solution)/shard_map/rows_line/ppermute | solution.py:437
  6.1 13.5 %collective-permute-start = (bf16[64,2176]{1,0:T(8,128)(2,1)S(1)}, bf16[64,2176]{1,0:T(8,128)(2,1)S(1)}, u32[]{:S(2)}, u32[]{:S(2)}) collective-permute-start(bf16[64,2176]{1,0:T(8,128)(2,1)S(1)} %get-tuple-element.160), channel_id=1, source_target_pairs={{0,4},{2,6},{4,0},{6,2},{8,12},{10,14},{12,8},{14,10},{1,5},{3,7},... | collective-permute-start | bytes 835592 | tf_op jit(solution)/shard_map/rows_line/ppermute | solution.py:437
  7.7 15.1 %copy-start = (bf16[128,2048]{1,0:T(8,128)(2,1)S(1)}, bf16[128,2048]{1,0:T(8,128)(2,1)}, u32[]{:S(2)}) copy-start(bf16[128,2048]{1,0:T(8,128)(2,1)} %rows) | copy-start | bytes 1572868
  19.7 12.6 %collective-permute-start.4 = (bf16[64,2176]{1,0:T(8,128)(2,1)S(1)}, bf16[64,2176]{1,0:T(8,128)(2,1)S(1)}, u32[]{:S(2)}, u32[]{:S(2)}) collective-permute-start(bf16[64,2176]{1,0:T(8,128)(2,1)S(1)} %collective-permute-done.1.refs_1_), channel_id=1, source_target_pairs={{0,4},{2,6},{4,0},{6,2},{8,12},{10,14},{12,8},{14,10},{1,5},{3,7},... | collective-permute-start | bytes 835592 | tf_op jit(solution)/shard_map/rows_line/ppermute | solution.py:437
  21.2 21.0 %collective-permute-start.3 = (bf16[128,2176]{1,0:T(8,128)(2,1)S(1)}, bf16[128,2176]{1,0:T(8,128)(2,1)S(1)}, u32[]{:S(2)}, u32[]{:S(2)}) collective-permute-start(bf16[128,2176]{1,0:T(8,128)(2,1)S(1)} %join.3.refs_0_.refs_1_), channel_id=1, source_target_pairs={{0,1},{1,0},{2,3},{3,2},{4,5},{5,4},{6,7},{7,6},{8,9},{9,8},{10,11... | collective-permute-start | bytes 1671176 | tf_op jit(solution)/shard_map/rows_across/ppermute | solution.py:445
  22.8 14.0 %collective-permute-start.6 = (bf16[64,2048]{1,0:T(8,128)(2,1)S(1)}, bf16[64,2048]{1,0:T(8,128)(2,1)S(1)}, u32[]{:S(2)}, u32[]{:S(2)}) collective-permute-start(bf16[64,2048]{1,0:T(8,128)(2,1)S(1)} %get-tuple-element.173), channel_id=1, source_target_pairs={{0,8},{2,10},{4,12},{6,14},{8,0},{10,2},{12,4},{14,6},{1,9},{3,11}... | collective-permute-start | bytes 786440 | tf_op jit(solution)/shard_map/grads_line/ppermute | solution.py:437
  32.3 10.0 %collective-permute-start.5 = (bf16[64,2176]{1,0:T(8,128)(2,1)S(1)}, bf16[64,2176]{1,0:T(8,128)(2,1)S(1)}, u32[]{:S(2)}, u32[]{:S(2)}) collective-permute-start(bf16[64,2176]{1,0:T(8,128)(2,1)S(1)} %collective-permute-done.4.refs_4_), channel_id=1, source_target_pairs={{0,1},{1,0},{2,3},{3,2},{4,5},{5,4},{6,7},{7,6},{8,9},{9,8},{10,11... | collective-permute-start | bytes 835592 | tf_op jit(solution)/shard_map/rows_across/ppermute | solution.py:445
  36.9 10.7 %collective-permute-start.9 = (bf16[64,2048]{1,0:T(8,128)(2,1)S(1)}, bf16[64,2048]{1,0:T(8,128)(2,1)S(1)}, u32[]{:S(2)}, u32[]{:S(2)}) collective-permute-start(bf16[64,2048]{1,0:T(8,128)(2,1)S(1)} %collective-permute-done.6.refs_1_), channel_id=1, source_target_pairs={{0,1},{1,0},{2,3},{3,2},{4,5},{5,4},{6,7},{7,6},{8,9},{9,8},{10,11... | collective-permute-start | bytes 786440 | tf_op jit(solution)/shard_map/grads_across/ppermute | solution.py:445
  37.4 10.2 %collective-permute-start.8 = (bf16[64,2048]{1,0:T(8,128)(2,1)S(1)}, bf16[64,2048]{1,0:T(8,128)(2,1)S(1)}, u32[]{:S(2)}, u32[]{:S(2)}) collective-permute-start(bf16[64,2048]{1,0:T(8,128)(2,1)S(1)} %collective-permute-done.6.refs_1_), channel_id=1, source_target_pairs={{0,4},{2,6},{4,0},{6,2},{8,12},{10,14},{12,8},{14,10},{1,5},{3,7},... | collective-permute-start | bytes 786440 | tf_op jit(solution)/shard_map/grads_line/ppermute | solution.py:437
  37.7 21.3 %collective-permute-start.12 = (bf16[128,2048]{1,0:T(8,128)(2,1)S(1)}, bf16[128,2048]{1,0:T(8,128)(2,1)S(1)}, u32[]{:S(2)}, u32[]{:S(2)}) collective-permute-start(bf16[128,2048]{1,0:T(8,128)(2,1)S(1)} %get-tuple-element.259.refs_0_), channel_id=1, source_target_pairs={{0,4},{2,6},{4,0},{6,2},{8,12},{10,14},{12,8},{14,10},{1,5},{3,7},... | collective-permute-start | bytes 1572872 | tf_op jit(solution)/shard_map/grads_line/ppermute | solution.py:437
  42.4 7.2 %collective-permute-start.7 = (bf16[384,2176]{1,0:T(8,128)(2,1)S(1)}, bf16[384,2176]{1,0:T(8,128)(2,1)S(1)}, u32[]{:S(2)}, u32[]{:S(2)}) collective-permute-start(bf16[384,2176]{1,0:T(8,128)(2,1)S(1)} %join.4.refs_1_.refs_3_), channel_id=1, source_target_pairs={{0,2},{2,0},{4,6},{6,4},{8,10},{10,8},{12,14},{14,12},{1,3},{3,1},... | collective-permute-start | bytes 5013512 | tf_op jit(solution)/shard_map/rows_cores/ppermute | solution.py:441
  47.0 12.0 %collective-permute-start.14 = (bf16[128,2048]{1,0:T(8,128)(2,1)S(1)}, bf16[128,2048]{1,0:T(8,128)(2,1)S(1)}, u32[]{:S(2)}, u32[]{:S(2)}) collective-permute-start(bf16[128,2048]{1,0:T(8,128)(2,1)S(1)} %get-tuple-element.259.refs_0_), channel_id=1, source_target_pairs={{0,2},{2,0},{4,6},{6,4},{8,10},{10,8},{12,14},{14,12},{1,3},{3,1},... | collective-permute-start | bytes 1572872 | tf_op jit(solution)/shard_map/grads_cores/ppermute | solution.py:441
  47.5 11.4 %collective-permute-start.13 = (bf16[64,2048]{1,0:T(8,128)(2,1)S(1)}, bf16[64,2048]{1,0:T(8,128)(2,1)S(1)}, u32[]{:S(2)}, u32[]{:S(2)}) collective-permute-start(bf16[64,2048]{1,0:T(8,128)(2,1)S(1)} %collective-permute-done.8.refs_4_), channel_id=1, source_target_pairs={{0,1},{1,0},{2,3},{3,2},{4,5},{5,4},{6,7},{7,6},{8,9},{9,8},{10,11... | collective-permute-start | bytes 786440 | tf_op jit(solution)/shard_map/grads_across/ppermute | solution.py:445
  56.5 2.7 %collective-permute-start.11 = (bf16[512,1024]{1,0:T(8,128)(2,1)S(1)}, bf16[512,1024]{1,0:T(8,128)(2,1)S(1)}, u32[]{:S(2)}, u32[]{:S(2)}) collective-permute-start(bf16[512,1024]{1,0:T(8,128)(2,1)S(1)} %get-tuple-element.201), channel_id=1, source_target_pairs={{0,2},{2,0},{4,6},{6,4},{8,10},{10,8},{12,14},{14,12},{1,3},{3,1},... | collective-permute-start | bytes 3145736 | tf_op jit(solution)/shard_map/out_cores/ppermute | solution.py:441
  59.4 3.9 %collective-permute-start.15 = (bf16[384,2048]{1,0:T(8,128)(2,1)S(1)}, bf16[384,2048]{1,0:T(8,128)(2,1)S(1)}, u32[]{:S(2)}, u32[]{:S(2)}) collective-permute-start(bf16[384,2048]{1,0:T(8,128)(2,1)S(1)} %join.5.refs_1_), channel_id=1, source_target_pairs={{0,2},{2,0},{4,6},{6,4},{8,10},{10,8},{12,14},{14,12},{1,3},{3,1},... | collective-permute-start | bytes 4718600 | tf_op jit(solution)/shard_map/grads_cores/ppermute | solution.py:441
  59.8 20.4 %collective-permute-start.10 = (bf16[512,1024]{1,0:T(8,128)(2,1)S(1)}, bf16[512,1024]{1,0:T(8,128)(2,1)S(1)}, u32[]{:S(2)}, u32[]{:S(2)}) collective-permute-start(bf16[512,1024]{1,0:T(8,128)(2,1)S(1)} %get-tuple-element.202), channel_id=1, source_target_pairs={{0,2},{2,0},{4,6},{6,4},{8,10},{10,8},{12,14},{14,12},{1,3},{3,1},... | collective-permute-start | bytes 3145736 | tf_op jit(solution)/shard_map/out_cores/ppermute | solution.py:441
  60.0 20.1 %collective-permute-start.19 = (bf16[384,1024]{1,0:T(8,128)(2,1)S(1)}, bf16[384,1024]{1,0:T(8,128)(2,1)S(1)}, u32[]{:S(2)}, u32[]{:S(2)}) collective-permute-start(bf16[384,1024]{1,0:T(8,128)(2,1)S(1)} %get-tuple-element.214), channel_id=1, source_target_pairs={{0,1},{1,0},{2,3},{3,2},{4,5},{5,4},{6,7},{7,6},{8,9},{9,8},{10,11... | collective-permute-start | bytes 2359304 | tf_op jit(solution)/shard_map/out_across/ppermute | solution.py:445
  71.1 5.1 %collective-permute-start.17 = (bf16[256,1152]{1,0:T(8,128)(2,1)S(1)}, bf16[256,1152]{1,0:T(8,128)(2,1)S(1)}, u32[]{:S(2)}, u32[]{:S(2)}) collective-permute-start(bf16[256,1152]{1,0:T(8,128)(2,1)S(1)} %get-tuple-element.243), channel_id=1, source_target_pairs={{0,2},{2,0},{4,6},{6,4},{8,10},{10,8},{12,14},{14,12},{1,3},{3,1},... | collective-permute-start | bytes 1769480 | tf_op jit(solution)/shard_map/in_cores/ppermute | solution.py:441
  71.4 24.4 %collective-permute-start.16 = (bf16[256,1152]{1,0:T(8,128)(2,1)S(1)}, bf16[256,1152]{1,0:T(8,128)(2,1)S(1)}, u32[]{:S(2)}, u32[]{:S(2)}) collective-permute-start(bf16[256,1152]{1,0:T(8,128)(2,1)S(1)} %get-tuple-element.245), channel_id=1, source_target_pairs={{0,2},{2,0},{4,6},{6,4},{8,10},{10,8},{12,14},{14,12},{1,3},{3,1},... | collective-permute-start | bytes 1769480 | tf_op jit(solution)/shard_map/in_cores/ppermute | solution.py:441
  76.3 19.5 %collective-permute-start.18 = (bf16[256,1152]{1,0:T(8,128)(2,1)S(1)}, bf16[256,1152]{1,0:T(8,128)(2,1)S(1)}, u32[]{:S(2)}, u32[]{:S(2)}) collective-permute-start(bf16[256,1152]{1,0:T(8,128)(2,1)S(1)} %in_send.2), channel_id=1, source_target_pairs={{0,1},{1,0},{2,3},{3,2},{4,5},{5,4},{6,7},{7,6},{8,9},{9,8},{10,11... | collective-permute-start | bytes 1769480 | tf_op jit(solution)/shard_map/in_across/ppermute | solution.py:445
  78.3 18.7 %collective-permute-start.24 = (bf16[256,1152]{1,0:T(8,128)(2,1)S(1)}, bf16[256,1152]{1,0:T(8,128)(2,1)S(1)}, u32[]{:S(2)}, u32[]{:S(2)}) collective-permute-start(bf16[256,1152]{1,0:T(8,128)(2,1)S(1)} %get-tuple-element.242), channel_id=1, source_target_pairs={{0,2},{2,0},{4,6},{6,4},{8,10},{10,8},{12,14},{14,12},{1,3},{3,1},... | collective-permute-start | bytes 1769480 | tf_op jit(solution)/shard_map/in_cores/ppermute | solution.py:441
  80.4 13.0 %collective-permute-start.20 = (bf16[256,1024]{1,0:T(8,128)(2,1)S(1)}, bf16[256,1024]{1,0:T(8,128)(2,1)S(1)}, u32[]{:S(2)}, u32[]{:S(2)}) collective-permute-start(bf16[256,1024]{1,0:T(8,128)(2,1)S(1)} %get-tuple-element.258), channel_id=1, source_target_pairs={{0,4},{2,6},{4,0},{6,2},{8,12},{10,14},{12,8},{14,10},{1,5},{3,7},... | collective-permute-start | bytes 1572872 | tf_op jit(solution)/shard_map/out_line/ppermute | solution.py:437
  80.5 30.1 %collective-permute-start.23 = (bf16[256,1152]{1,0:T(8,128)(2,1)S(1)}, bf16[256,1152]{1,0:T(8,128)(2,1)S(1)}, u32[]{:S(2)}, u32[]{:S(2)}) collective-permute-start(bf16[256,1152]{1,0:T(8,128)(2,1)S(1)} %get-tuple-element.244), channel_id=1, source_target_pairs={{0,2},{2,0},{4,6},{6,4},{8,10},{10,8},{12,14},{14,12},{1,3},{3,1},... | collective-permute-start | bytes 1769480 | tf_op jit(solution)/shard_map/in_cores/ppermute | solution.py:441
  93.4 18.0 %collective-permute-start.22 = (bf16[128,1024]{1,0:T(8,128)(2,1)S(1)}, bf16[128,1024]{1,0:T(8,128)(2,1)S(1)}, u32[]{:S(2)}, u32[]{:S(2)}) collective-permute-start(bf16[128,1024]{1,0:T(8,128)(2,1)S(1)} %add_last.1), channel_id=1, source_target_pairs={{0,8},{2,10},{4,12},{6,14},{8,0},{10,2},{12,4},{14,6},{1,9},{3,11}... | collective-permute-start | bytes 786440 | tf_op jit(solution)/shard_map/out_line/ppermute | solution.py:437
  95.9 14.4 %collective-permute-start.26 = (bf16[128,1152]{1,0:T(8,128)(2,1)S(1)}, bf16[128,1152]{1,0:T(8,128)(2,1)S(1)}, u32[]{:S(2)}, u32[]{:S(2)}) collective-permute-start(bf16[128,1152]{1,0:T(8,128)(2,1)S(1)} %in_slot.3), channel_id=1, source_target_pairs={{0,4},{2,6},{4,0},{6,2},{8,12},{10,14},{12,8},{14,10},{1,5},{3,7},... | collective-permute-start | bytes 884744 | tf_op jit(solution)/shard_map/in_line/ppermute | solution.py:437
  97.1 13.4 %collective-permute-start.25 = (bf16[128,1152]{1,0:T(8,128)(2,1)S(1)}, bf16[128,1152]{1,0:T(8,128)(2,1)S(1)}, u32[]{:S(2)}, u32[]{:S(2)}) collective-permute-start(bf16[128,1152]{1,0:T(8,128)(2,1)S(1)} %get-tuple-element.273), channel_id=1, source_target_pairs={{0,1},{1,0},{2,3},{3,2},{4,5},{5,4},{6,7},{7,6},{8,9},{9,8},{10,11... | collective-permute-start | bytes 884744 | tf_op jit(solution)/shard_map/in_across/ppermute | solution.py:445
  97.8 12.8 %collective-permute-start.21 = (bf16[128,1024]{1,0:T(8,128)(2,1)S(1)}, bf16[128,1024]{1,0:T(8,128)(2,1)S(1)}, u32[]{:S(2)}, u32[]{:S(2)}) collective-permute-start(bf16[128,1024]{1,0:T(8,128)(2,1)S(1)} %get-tuple-element.270), channel_id=1, source_target_pairs={{0,1},{1,0},{2,3},{3,2},{4,5},{5,4},{6,7},{7,6},{8,9},{9,8},{10,11... | collective-permute-start | bytes 786440 | tf_op jit(solution)/shard_map/out_across/ppermute | solution.py:445
  110.5 10.5 %collective-permute-start.27 = (bf16[128,1152]{1,0:T(8,128)(2,1)S(1)}, bf16[128,1152]{1,0:T(8,128)(2,1)S(1)}, u32[]{:S(2)}, u32[]{:S(2)}) collective-permute-start(bf16[128,1152]{1,0:T(8,128)(2,1)S(1)} %in_slot.4), channel_id=1, source_target_pairs={{0,8},{2,10},{4,12},{6,14},{8,0},{10,2},{12,4},{14,6},{1,9},{3,11}... | collective-permute-start | bytes 884744 | tf_op jit(solution)/shard_map/in_line/ppermute | solution.py:437
  110.7 10.3 %collective-permute-start.29 = (bf16[128,1152]{1,0:T(8,128)(2,1)S(1)}, bf16[128,1152]{1,0:T(8,128)(2,1)S(1)}, u32[]{:S(2)}, u32[]{:S(2)}) collective-permute-start(bf16[128,1152]{1,0:T(8,128)(2,1)S(1)} %get-tuple-element.302), channel_id=1, source_target_pairs={{0,1},{1,0},{2,3},{3,2},{4,5},{5,4},{6,7},{7,6},{8,9},{9,8},{10,11... | collective-permute-start | bytes 884744 | tf_op jit(solution)/shard_map/in_across/ppermute | solution.py:445
  111.2 10.0 %collective-permute-start.28 = (bf16[128,1152]{1,0:T(8,128)(2,1)S(1)}, bf16[128,1152]{1,0:T(8,128)(2,1)S(1)}, u32[]{:S(2)}, u32[]{:S(2)}) collective-permute-start(bf16[128,1152]{1,0:T(8,128)(2,1)S(1)} %in_slot.5), channel_id=1, source_target_pairs={{0,4},{2,6},{4,0},{6,2},{8,12},{10,14},{12,8},{14,10},{1,5},{3,7},... | collective-permute-start | bytes 884744 | tf_op jit(solution)/shard_map/in_line/ppermute | solution.py:437
  118.5 2.7 %copy-start.1 = (s32[128,4]{0,1:T(4,128)S(1)}, s32[128,4]{0,1:T(4,128)}, u32[]{:S(2)}) copy-start(s32[128,4]{0,1:T(4,128)} %param.9) | copy-start | bytes 6148
  118.5 2.7 %copy-start.2 = (f32[128,4]{0,1:T(4,128)S(1)}, f32[128,4]{0,1:T(4,128)}, u32[]{:S(2)}) copy-start(f32[128,4]{0,1:T(4,128)} %param.11) | copy-start | bytes 6148
  118.6 2.7 %copy-start.3 = (s32[128]{0:T(128)S(1)}, s32[128]{0:T(128)}, u32[]{:S(2)}) copy-start(s32[128]{0:T(128)} %param.10) | copy-start | bytes 1540

commit v2 on v1

--- a/solution.py
+++ b/solution.py
@@ -206,7 +206,7 @@
     pre = jax.ShapeDtypeStruct((total, hidden), jnp.float32)
     act = jax.ShapeDtypeStruct((total, hidden), jnp.bfloat16)
     return call(
-        functools.partial(hidden_kernel, experts, 256),
+        functools.partial(hidden_kernel, experts, 512),
         "hidden_units",
         (*pieces, gate_mat, up_mat),
         (pre, pre, act),
@@ -232,7 +232,7 @@
     width = down_mat.shape[1]
     sums = jax.ShapeDtypeStruct((total, width // 2), jnp.bfloat16)
     return call(
-        functools.partial(outputs_kernel, 256), "outputs", (gated, down_mat), (sums, sums)
+        functools.partial(outputs_kernel, 512), "outputs", (gated, down_mat), (sums, sums)
     )
 
 
@@ -265,7 +265,7 @@
     total = pre_gate.shape[0]
     act = jax.ShapeDtypeStruct((total, hidden), jnp.bfloat16)
     return call(
-        functools.partial(hidden_grads_kernel, experts, 256),
+        functools.partial(hidden_grads_kernel, experts, 512),
         "hidden_grads",
         (*pieces, *gate_pieces, down_mat, pre_gate, pre_up),
         (act, act, jax.ShapeDtypeStruct((total, LANES), jnp.bfloat16)),
@@ -299,7 +299,7 @@
     total = d_gate.shape[0]
     sums = jax.ShapeDtypeStruct((total // split, width // 2 + LANES), jnp.bfloat16)
     return call(
-        functools.partial(input_grads_kernel, 256),
+        functools.partial(input_grads_kernel, 512),
         "input_grads",
         (d_gate, d_up, shares, gate_mat, up_mat),
         (sums,) * (2 * split),

time: 123 us -> 122 us (level)
  transfers between devices with their start and end apart: 30 -> 30, of which waited for: 11 -> 11; matrix products, arithmetic and copies ran while one was open for 0% -> 0% of each run, Pallas kernels for 45% -> 44%
where the time goes in v2:
time: 122 us
  Pallas kernels  57 us (47%)
  waiting for transfers between devices  35.5 us (29%)
  starting transfers between devices  28.7 us (24%)
    pallas_call x22, Pallas kernels, call(): pl.pallas_call(kernel, out_shape=out_shape, in_specs=[VMEM] * len(operand...  32.5 us
    ppermute x11, waiting for transfers between devices, line(): return lax.ppermute(array, 'expert', pairs)  30.6 us
    pallas_call x3, Pallas kernels, weights(): pl.pallas_call(functools.partial(weights_kernel, width, 512), out_shape=j...  18.5 us
    ppermute x11, starting transfers between devices, line(): return lax.ppermute(array, 'expert', pairs)  15.1 us
    ppermute x9, starting transfers between devices, across(): return lax.ppermute(array, 'helper', self.sides)  11.2 us
    pallas_call x1, Pallas kernels, load(): pl.pallas_call(load_kernel, out_shape=tuple((jax.ShapeDtypeStruct(mat.sha...  4.73 us
    ppermute x9, waiting for transfers between devices, across(): return lax.ppermute(array, 'helper', self.sides)  4.67 us
  transfers between devices with their start and end apart: 30, of which 11 were waited for; matrix products, arithmetic and copies ran while one was open for 0% of the time, Pallas kernels for 44%

profile of v2, /device:TPU:0, one launch (start us, length us, event | category | flops | bytes accessed | tf_op | source)
XLA Modules:
  0.0 122.2 jit_solution(13858802391035714239)
XLA Ops:
  0.6 1.3 %prepare_rows.1 = (bf16[64,2176]{1,0:T(8,128)(2,1)S(1)}, bf16[128,2176]{1,0:T(8,128)(2,1)S(1)}, f32[8,128]{1,0:T(8,128)S(1)}) custom-call(s32[4,128]{1,0:T(4,128)} %bitcast.10, s32[1,128]{1,0:T(1,128)} %bitcast.14, f32[4,128]{1,0:T(4,128)} %bitcast.12, bf16[128,2048]{1,0:T(8,128)(2,1)} %refs_3_.1), custom_call_target="tpu_custom_call" | custom-call | tf_op jit(solution)/shard_map/prepare_rows/pallas_call | solution.py:112
  1.9 0.5 collective-permute-start.2
  2.5 3.7 %collective-permute-start.1 = (bf16[64,2176]{1,0:T(8,128)(2,1)S(1)}, bf16[64,2176]{1,0:T(8,128)(2,1)S(1)}, u32[]{:S(2)}, u32[]{:S(2)}) collective-permute-start(bf16[64,2176]{1,0:T(8,128)(2,1)S(1)} %get-tuple-element.160), channel_id=1, source_target_pairs={{0,8},{2,10},{4,12},{6,14},{8,0},{10,2},{12,4},{14,6},{1,9},{3,11}... | collective-permute-start | bytes 835592 | tf_op jit(solution)/shard_map/rows_line/ppermute | solution.py:437
  6.1 1.6 %collective-permute-start = (bf16[64,2176]{1,0:T(8,128)(2,1)S(1)}, bf16[64,2176]{1,0:T(8,128)(2,1)S(1)}, u32[]{:S(2)}, u32[]{:S(2)}) collective-permute-start(bf16[64,2176]{1,0:T(8,128)(2,1)S(1)} %get-tuple-element.160), channel_id=1, source_target_pairs={{0,4},{2,6},{4,0},{6,2},{8,12},{10,14},{12,8},{14,10},{1,5},{3,7},... | collective-permute-start | bytes 835592 | tf_op jit(solution)/shard_map/rows_line/ppermute | solution.py:437
  7.7 4.7 %load.1 = (bf16[2048,1024]{1,0:T(8,128)(2,1)S(1)}, bf16[2048,1024]{1,0:T(8,128)(2,1)S(1)}, bf16[1024,2048]{1,0:T(8,128)(2,1)S(1)}) custom-call(bf16[2048,1024]{1,0:T(8,128)(2,1)} %bitcast.16, bf16[2048,1024]{1,0:T(8,128)(2,1)} %bitcast.17, bf16[1024,2048]{1,0:T(8,128)(2,1)} %bitcast.18), custom_call_target="tpu_custom_call" | custom-call | tf_op jit(solution)/shard_map/load/pallas_call | solution.py:488
  12.4 7.0 %collective-permute-done.1.refs_1_ = bf16[64,2176]{1,0:T(8,128)(2,1)S(1)} collective-permute-done((bf16[64,2176]{1,0:T(8,128)(2,1)S(1)}, bf16[64,2176]{1,0:T(8,128)(2,1)S(1)}, u32[]{:S(2)}, u32[]{:S(2)}) %collective-permute-start.1) | collective-permute-done | bytes 278560 | tf_op jit(solution)/shard_map/rows_line/ppermute | solution.py:437
  19.7 1.6 %collective-permute-start.4 = (bf16[64,2176]{1,0:T(8,128)(2,1)S(1)}, bf16[64,2176]{1,0:T(8,128)(2,1)S(1)}, u32[]{:S(2)}, u32[]{:S(2)}) collective-permute-start(bf16[64,2176]{1,0:T(8,128)(2,1)S(1)} %collective-permute-done.1.refs_1_), channel_id=1, source_target_pairs={{0,4},{2,6},{4,0},{6,2},{8,12},{10,14},{12,8},{14,10},{1,5},{3,7},... | collective-permute-start | bytes 835592 | tf_op jit(solution)/shard_map/rows_line/ppermute | solution.py:437
  21.2 1.5 %collective-permute-start.3 = (bf16[128,2176]{1,0:T(8,128)(2,1)S(1)}, bf16[128,2176]{1,0:T(8,128)(2,1)S(1)}, u32[]{:S(2)}, u32[]{:S(2)}) collective-permute-start(bf16[128,2176]{1,0:T(8,128)(2,1)S(1)} %join.3.refs_0_.refs_1_), channel_id=1, source_target_pairs={{0,1},{1,0},{2,3},{3,2},{4,5},{5,4},{6,7},{7,6},{8,9},{9,8},{10,11... | collective-permute-start | bytes 1671176 | tf_op jit(solution)/shard_map/rows_across/ppermute | solution.py:445
  22.8 2.4 %collective-permute-start.6 = (bf16[64,2048]{1,0:T(8,128)(2,1)S(1)}, bf16[64,2048]{1,0:T(8,128)(2,1)S(1)}, u32[]{:S(2)}, u32[]{:S(2)}) collective-permute-start(bf16[64,2048]{1,0:T(8,128)(2,1)S(1)} %get-tuple-element.173), channel_id=1, source_target_pairs={{0,8},{2,10},{4,12},{6,14},{8,0},{10,2},{12,4},{14,6},{1,9},{3,11}... | collective-permute-start | bytes 786440 | tf_op jit(solution)/shard_map/grads_line/ppermute | solution.py:437
  25.2 7.1 %collective-permute-done.4.refs_4_ = bf16[64,2176]{1,0:T(8,128)(2,1)S(1)} collective-permute-done((bf16[64,2176]{1,0:T(8,128)(2,1)S(1)}, bf16[64,2176]{1,0:T(8,128)(2,1)S(1)}, u32[]{:S(2)}, u32[]{:S(2)}) %collective-permute-start.4) | collective-permute-done | bytes 278560 | tf_op jit(solution)/shard_map/rows_line/ppermute | solution.py:437
  32.3 2.4 %collective-permute-start.5 = (bf16[64,2176]{1,0:T(8,128)(2,1)S(1)}, bf16[64,2176]{1,0:T(8,128)(2,1)S(1)}, u32[]{:S(2)}, u32[]{:S(2)}) collective-permute-start(bf16[64,2176]{1,0:T(8,128)(2,1)S(1)} %collective-permute-done.4.refs_4_), channel_id=1, source_target_pairs={{0,1},{1,0},{2,3},{3,2},{4,5},{5,4},{6,7},{7,6},{8,9},{9,8},{10,11... | collective-permute-start | bytes 835592 | tf_op jit(solution)/shard_map/rows_across/ppermute | solution.py:445
  34.7 2.2 %collective-permute-done.6.refs_1_ = bf16[64,2048]{1,0:T(8,128)(2,1)S(1)} collective-permute-done((bf16[64,2048]{1,0:T(8,128)(2,1)S(1)}, bf16[64,2048]{1,0:T(8,128)(2,1)S(1)}, u32[]{:S(2)}, u32[]{:S(2)}) %collective-permute-start.6) | collective-permute-done | bytes 262176 | tf_op jit(solution)/shard_map/grads_line/ppermute | solution.py:437
  36.9 0.5 collective-permute-start.9
  37.4 0.3 collective-permute-start.8
  37.7 1.7 %collective-permute-start.12 = (bf16[128,2048]{1,0:T(8,128)(2,1)S(1)}, bf16[128,2048]{1,0:T(8,128)(2,1)S(1)}, u32[]{:S(2)}, u32[]{:S(2)}) collective-permute-start(bf16[128,2048]{1,0:T(8,128)(2,1)S(1)} %get-tuple-element.259.refs_0_), channel_id=1, source_target_pairs={{0,4},{2,6},{4,0},{6,2},{8,12},{10,14},{12,8},{14,10},{1,5},{3,7},... | collective-permute-start | bytes 1572872 | tf_op jit(solution)/shard_map/grads_line/ppermute | solution.py:437
  39.4 2.9 %collective-permute-done.5.refs_5_ = bf16[64,2176]{1,0:T(8,128)(2,1)S(1)} collective-permute-done((bf16[64,2176]{1,0:T(8,128)(2,1)S(1)}, bf16[64,2176]{1,0:T(8,128)(2,1)S(1)}, u32[]{:S(2)}, u32[]{:S(2)}) %collective-permute-start.5) | collective-permute-done | bytes 278560 | tf_op jit(solution)/shard_map/rows_across/ppermute | solution.py:445
  42.5 4.5 %hidden_units.2 = (f32[512,1024]{1,0:T(8,128)S(1)}, f32[512,1024]{1,0:T(8,128)S(1)}, bf16[512,1024]{1,0:T(8,128)(2,1)S(1)}) custom-call(bf16[128,2176]{1,0:T(8,128)(2,1)S(1)} %get-tuple-element.295.refs_0_.refs_2_, bf16[384,2176]{1,0:T(8,128)(2,1)S(1)} %join.4.refs_1_.refs_3_, bf16[2048,1024]{1,0:T(8,128)(2,1)S(1)} %get-tuple-element.165.refs_2_.gate_mat, ...), custom_call_target="tpu_custom_call" | custom-call | flops 4294967296 | tf_op jit(solution)/shard_map/hidden_units/pallas_call | solution.py:40
  47.0 0.6 collective-permute-start.14
  47.5 2.0 %collective-permute-start.13 = (bf16[64,2048]{1,0:T(8,128)(2,1)S(1)}, bf16[64,2048]{1,0:T(8,128)(2,1)S(1)}, u32[]{:S(2)}, u32[]{:S(2)}) collective-permute-start(bf16[64,2048]{1,0:T(8,128)(2,1)S(1)} %collective-permute-done.8.refs_4_), channel_id=1, source_target_pairs={{0,1},{1,0},{2,3},{3,2},{4,5},{5,4},{6,7},{7,6},{8,9},{9,8},{10,11... | collective-permute-start | bytes 786440 | tf_op jit(solution)/shard_map/grads_across/ppermute | solution.py:445
  49.6 4.5 %hidden_units.3 = (f32[512,1024]{1,0:T(8,128)S(1)}, f32[512,1024]{1,0:T(8,128)S(1)}, bf16[512,1024]{1,0:T(8,128)(2,1)S(1)}) custom-call(bf16[128,2176]{1,0:T(8,128)(2,1)S(1)} %collective-permute-done.2.refs_0_.refs_2_, bf16[384,2176]{1,0:T(8,128)(2,1)S(1)} %collective-permute-done.7.refs_1_.refs_3_, ...), custom_call_target="tpu_custom_call" | custom-call | flops 4294967296 | tf_op jit(solution)/shard_map/hidden_units/pallas_call | solution.py:40
  54.1 2.4 %outputs.2 = (bf16[512,1024]{1,0:T(8,128)(2,1)S(1)}, bf16[512,1024]{1,0:T(8,128)(2,1)S(1)}) custom-call(bf16[512,1024]{1,0:T(8,128)(2,1)S(1)} %get-tuple-element.264.gated.refs_5_, bf16[1024,2048]{1,0:T(8,128)(2,1)S(1)} %get-tuple-element.204.down_mat.refs_4_), custom_call_target="tpu_custom_call" | custom-call | tf_op jit(solution)/shard_map/outputs/pallas_call | solution.py:40
  56.5 2.4 %outputs.3 = (bf16[512,1024]{1,0:T(8,128)(2,1)S(1)}, bf16[512,1024]{1,0:T(8,128)(2,1)S(1)}) custom-call(bf16[512,1024]{1,0:T(8,128)(2,1)S(1)} %get-tuple-element.263.gated.refs_4_, bf16[1024,2048]{1,0:T(8,128)(2,1)S(1)} %get-tuple-element.204.down_mat.refs_4_), custom_call_target="tpu_custom_call" | custom-call | tf_op jit(solution)/shard_map/outputs/pallas_call | solution.py:40
  59.0 0.2 collective-permute-done.11.received
  59.4 0.3 collective-permute-start.15
  59.7 0.2 collective-permute-start.10
  60.0 3.3 %hidden_grads.2 = (bf16[512,1024]{1,0:T(8,128)(2,1)S(1)}, bf16[512,1024]{1,0:T(8,128)(2,1)S(1)}, bf16[512,128]{1,0:T(8,128)(2,1)S(1)}) custom-call(bf16[128,2048]{1,0:T(8,128)(2,1)S(1)} %get-tuple-element.259.refs_0_, bf16[384,2048]{1,0:T(8,128)(2,1)S(1)} %join.5.refs_1_, bf16[128,2176]{1,0:T(8,128)(2,1)S(1)} %get-tuple-element.295.refs_0_.refs_2_, ...), custom_call_target="tpu_custom_call" | custom-call | tf_op jit(solution)/shard_map/hidden_grads/pallas_call | solution.py:40
  63.3 3.1 %hidden_grads.3 = (bf16[512,1024]{1,0:T(8,128)(2,1)S(1)}, bf16[512,1024]{1,0:T(8,128)(2,1)S(1)}, bf16[512,128]{1,0:T(8,128)(2,1)S(1)}) custom-call(bf16[128,2048]{1,0:T(8,128)(2,1)S(1)} %collective-permute-done.14.refs_0_.refs_2_, bf16[384,2048]{1,0:T(8,128)(2,1)S(1)} %collective-permute-done.15.refs_1_.refs_3_, ...), custom_call_target="tpu_custom_call" | custom-call | tf_op jit(solution)/shard_map/hidden_grads/pallas_call | solution.py:40
  66.5 4.5 %input_grads.2 = (bf16[256,1152]{1,0:T(8,128)(2,1)S(1)}, bf16[256,1152]{1,0:T(8,128)(2,1)S(1)}, bf16[256,1152]{1,0:T(8,128)(2,1)S(1)}, bf16[256,1152]{1,0:T(8,128)(2,1)S(1)}) custom-call(bf16[512,1024]{1,0:T(8,128)(2,1)S(1)} %get-tuple-element.280.d_gate.refs_5_, bf16[512,1024]{1,0:T(8,128)(2,1)S(1)} %get-tuple-element.300.d_up.refs_5_, ...), custom_call_target="tpu_custom_call" | custom-call | tf_op jit(solution)/shard_map/input_grads/pallas_call | solution.py:40
  71.0 0.3 collective-permute-start.17
  71.4 0.2 collective-permute-start.16
  71.6 4.5 %input_grads.3 = (bf16[512,1152]{1,0:T(8,128)(2,1)S(1)}, bf16[512,1152]{1,0:T(8,128)(2,1)S(1)}) custom-call(bf16[512,1024]{1,0:T(8,128)(2,1)S(1)} %get-tuple-element.279.d_gate.refs_4_, bf16[512,1024]{1,0:T(8,128)(2,1)S(1)} %get-tuple-element.299.d_up.refs_4_, bf16[512,128]{1,0:T(8,128)(2,1)S(1)} %get-tuple-element.248.shares, ...), custom_call_target="tpu_custom_call" | custom-call | tf_op jit(solution)/shard_map/input_grads/pallas_call | solution.py:40
  76.2 2.1 %collective-permute-start.18 = (bf16[256,1152]{1,0:T(8,128)(2,1)S(1)}, bf16[256,1152]{1,0:T(8,128)(2,1)S(1)}, u32[]{:S(2)}, u32[]{:S(2)}) collective-permute-start(bf16[256,1152]{1,0:T(8,128)(2,1)S(1)} %in_send.2), channel_id=1, source_target_pairs={{0,1},{1,0},{2,3},{3,2},{4,5},{5,4},{6,7},{7,6},{8,9},{9,8},{10,11... | collective-permute-start | bytes 1769480 | tf_op jit(solution)/shard_map/in_across/ppermute | solution.py:445
  78.3 1.8 %collective-permute-done.19.arrived = bf16[384,1024]{1,0:T(8,128)(2,1)S(1)} collective-permute-done((bf16[384,1024]{1,0:T(8,128)(2,1)S(1)}, bf16[384,1024]{1,0:T(8,128)(2,1)S(1)}, u32[]{:S(2)}, u32[]{:S(2)}) %collective-permute-start.19) | collective-permute-done | bytes 786464 | tf_op jit(solution)/shard_map/out_across/ppermute | solution.py:445
  80.1 0.3 out_slots.1
  80.5 6.1 %grad_down.1 = bf16[1024,2048]{1,0:T(8,128)(2,1)} custom-call(bf16[128,2048]{1,0:T(8,128)(2,1)S(1)} %get-tuple-element.259.refs_0_, bf16[384,2048]{1,0:T(8,128)(2,1)S(1)} %join.5.refs_1_, bf16[128,2048]{1,0:T(8,128)(2,1)S(1)} %collective-permute-done.14.refs_0_.refs_2_, bf16[384,2048]{1,0:T(8,128)(2,1)S(1)} %collective-permute-done.15.refs_1_.refs_3_, ...), custom_call_target="tpu_custom_call" | custom-call | flops 4294967296 | tf_op jit(solution)/shard_map/grad_down/pallas_call | solution.py:340
  86.7 6.7 %collective-permute-done.20.arrived.near_and_last = bf16[256,1024]{1,0:T(8,128)(2,1)S(1)} collective-permute-done((bf16[256,1024]{1,0:T(8,128)(2,1)S(1)}, bf16[256,1024]{1,0:T(8,128)(2,1)S(1)}, u32[]{:S(2)}, u32[]{:S(2)}) %collective-permute-start.20) | collective-permute-done | bytes 524320 | tf_op jit(solution)/shard_map/out_line/ppermute | solution.py:437
  93.4 2.4 %collective-permute-start.22 = (bf16[128,1024]{1,0:T(8,128)(2,1)S(1)}, bf16[128,1024]{1,0:T(8,128)(2,1)S(1)}, u32[]{:S(2)}, u32[]{:S(2)}) collective-permute-start(bf16[128,1024]{1,0:T(8,128)(2,1)S(1)} %add_last.1), channel_id=1, source_target_pairs={{0,8},{2,10},{4,12},{6,14},{8,0},{10,2},{12,4},{14,6},{1,9},{3,11}... | collective-permute-start | bytes 786440 | tf_op jit(solution)/shard_map/out_line/ppermute | solution.py:437
  95.8 1.1 collective-permute-start.26
  97.1 0.7 collective-permute-start.25
  97.7 1.4 %collective-permute-start.21 = (bf16[128,1024]{1,0:T(8,128)(2,1)S(1)}, bf16[128,1024]{1,0:T(8,128)(2,1)S(1)}, u32[]{:S(2)}, u32[]{:S(2)}) collective-permute-start(bf16[128,1024]{1,0:T(8,128)(2,1)S(1)} %get-tuple-element.270), channel_id=1, source_target_pairs={{0,1},{1,0},{2,3},{3,2},{4,5},{5,4},{6,7},{7,6},{8,9},{9,8},{10,11... | collective-permute-start | bytes 786440 | tf_op jit(solution)/shard_map/out_across/ppermute | solution.py:445
  99.1 6.2 %grad_gate.1 = bf16[2048,1024]{1,0:T(8,128)(2,1)} custom-call(bf16[128,2176]{1,0:T(8,128)(2,1)S(1)} %get-tuple-element.295.refs_0_.refs_2_, bf16[384,2176]{1,0:T(8,128)(2,1)S(1)} %join.4.refs_1_.refs_3_, bf16[128,2176]{1,0:T(8,128)(2,1)S(1)} %collective-permute-done.2.refs_0_.refs_2_, bf16[384,2176]{1,0:T(8,128)(2,1)S(1)} %collective-permute-done.7.refs_1_.refs_3_, ...), custom_call_target="tpu_custom_call" | custom-call | flops 4294967296 | tf_op jit(solution)/shard_map/grad_gate/pallas_call | solution.py:340
  105.3 4.9 %collective-permute-done.26.refs_0_ = bf16[128,1152]{1,0:T(8,128)(2,1)S(1)} collective-permute-done((bf16[128,1152]{1,0:T(8,128)(2,1)S(1)}, bf16[128,1152]{1,0:T(8,128)(2,1)S(1)}, u32[]{:S(2)}, u32[]{:S(2)}) %collective-permute-start.26) | collective-permute-done | bytes 294944 | tf_op jit(solution)/shard_map/in_line/ppermute | solution.py:437
  110.6 0.6 collective-permute-start.29
  111.4 0.9 finish_outputs.1
  112.3 6.2 %grad_up.1 = bf16[2048,1024]{1,0:T(8,128)(2,1)} custom-call(bf16[128,2176]{1,0:T(8,128)(2,1)S(1)} %get-tuple-element.295.refs_0_.refs_2_, bf16[384,2176]{1,0:T(8,128)(2,1)S(1)} %join.4.refs_1_.refs_3_, bf16[128,2176]{1,0:T(8,128)(2,1)S(1)} %collective-permute-done.2.refs_0_.refs_2_, bf16[384,2176]{1,0:T(8,128)(2,1)S(1)} %collective-permute-done.7.refs_1_.refs_3_, ...), custom_call_target="tpu_custom_call" | custom-call | tf_op jit(solution)/shard_map/grad_up/pallas_call | solution.py:340
  118.5 2.4 %collective-permute-done.27.refs_0_ = bf16[128,1152]{1,0:T(8,128)(2,1)S(1)} collective-permute-done((bf16[128,1152]{1,0:T(8,128)(2,1)S(1)}, bf16[128,1152]{1,0:T(8,128)(2,1)S(1)}, u32[]{:S(2)}, u32[]{:S(2)}) %collective-permute-start.27) | collective-permute-done | bytes 294944 | tf_op jit(solution)/shard_map/in_line/ppermute | solution.py:437
  120.9 0.3 collective-permute-done.28.refs_1_
  121.1 1.1 finish_inputs.1
  (52 shorter events, 1.8 us)
Async XLA Ops:
  1.9 10.5 %collective-permute-start.2 = (bf16[128,2176]{1,0:T(8,128)(2,1)S(1)}, bf16[128,2176]{1,0:T(8,128)(2,1)S(1)}, u32[]{:S(2)}, u32[]{:S(2)}) collective-permute-start(bf16[128,2176]{1,0:T(8,128)(2,1)S(1)} %get-tuple-element.295.refs_0_.refs_2_), channel_id=1, source_target_pairs={{0,2},{2,0},{4,6},{6,4},{8,10},{10,8},{12,14},{14,12},{1,3},{3,1},... | collective-permute-start | bytes 1671176 | tf_op jit(solution)/shard_map/rows_cores/ppermute | solution.py:441
  2.5 17.0 %collective-permute-start.1 = (bf16[64,2176]{1,0:T(8,128)(2,1)S(1)}, bf16[64,2176]{1,0:T(8,128)(2,1)S(1)}, u32[]{:S(2)}, u32[]{:S(2)}) collective-permute-start(bf16[64,2176]{1,0:T(8,128)(2,1)S(1)} %get-tuple-element.160), channel_id=1, source_target_pairs={{0,8},{2,10},{4,12},{6,14},{8,0},{10,2},{12,4},{14,6},{1,9},{3,11}... | collective-permute-start | bytes 835592 | tf_op jit(solution)/shard_map/rows_line/ppermute | solution.py:437
  6.1 13.5 %collective-permute-start = (bf16[64,2176]{1,0:T(8,128)(2,1)S(1)}, bf16[64,2176]{1,0:T(8,128)(2,1)S(1)}, u32[]{:S(2)}, u32[]{:S(2)}) collective-permute-start(bf16[64,2176]{1,0:T(8,128)(2,1)S(1)} %get-tuple-element.160), channel_id=1, source_target_pairs={{0,4},{2,6},{4,0},{6,2},{8,12},{10,14},{12,8},{14,10},{1,5},{3,7},... | collective-permute-start | bytes 835592 | tf_op jit(solution)/shard_map/rows_line/ppermute | solution.py:437
  7.7 15.1 %copy-start = (bf16[128,2048]{1,0:T(8,128)(2,1)S(1)}, bf16[128,2048]{1,0:T(8,128)(2,1)}, u32[]{:S(2)}) copy-start(bf16[128,2048]{1,0:T(8,128)(2,1)} %rows) | copy-start | bytes 1572868
  19.7 12.6 %collective-permute-start.4 = (bf16[64,2176]{1,0:T(8,128)(2,1)S(1)}, bf16[64,2176]{1,0:T(8,128)(2,1)S(1)}, u32[]{:S(2)}, u32[]{:S(2)}) collective-permute-start(bf16[64,2176]{1,0:T(8,128)(2,1)S(1)} %collective-permute-done.1.refs_1_), channel_id=1, source_target_pairs={{0,4},{2,6},{4,0},{6,2},{8,12},{10,14},{12,8},{14,10},{1,5},{3,7},... | collective-permute-start | bytes 835592 | tf_op jit(solution)/shard_map/rows_line/ppermute | solution.py:437
  21.2 21.0 %collective-permute-start.3 = (bf16[128,2176]{1,0:T(8,128)(2,1)S(1)}, bf16[128,2176]{1,0:T(8,128)(2,1)S(1)}, u32[]{:S(2)}, u32[]{:S(2)}) collective-permute-start(bf16[128,2176]{1,0:T(8,128)(2,1)S(1)} %join.3.refs_0_.refs_1_), channel_id=1, source_target_pairs={{0,1},{1,0},{2,3},{3,2},{4,5},{5,4},{6,7},{7,6},{8,9},{9,8},{10,11... | collective-permute-start | bytes 1671176 | tf_op jit(solution)/shard_map/rows_across/ppermute | solution.py:445
  22.8 14.0 %collective-permute-start.6 = (bf16[64,2048]{1,0:T(8,128)(2,1)S(1)}, bf16[64,2048]{1,0:T(8,128)(2,1)S(1)}, u32[]{:S(2)}, u32[]{:S(2)}) collective-permute-start(bf16[64,2048]{1,0:T(8,128)(2,1)S(1)} %get-tuple-element.173), channel_id=1, source_target_pairs={{0,8},{2,10},{4,12},{6,14},{8,0},{10,2},{12,4},{14,6},{1,9},{3,11}... | collective-permute-start | bytes 786440 | tf_op jit(solution)/shard_map/grads_line/ppermute | solution.py:437
  32.3 10.0 %collective-permute-start.5 = (bf16[64,2176]{1,0:T(8,128)(2,1)S(1)}, bf16[64,2176]{1,0:T(8,128)(2,1)S(1)}, u32[]{:S(2)}, u32[]{:S(2)}) collective-permute-start(bf16[64,2176]{1,0:T(8,128)(2,1)S(1)} %collective-permute-done.4.refs_4_), channel_id=1, source_target_pairs={{0,1},{1,0},{2,3},{3,2},{4,5},{5,4},{6,7},{7,6},{8,9},{9,8},{10,11... | collective-permute-start | bytes 835592 | tf_op jit(solution)/shard_map/rows_across/ppermute | solution.py:445
  36.9 10.7 %collective-permute-start.9 = (bf16[64,2048]{1,0:T(8,128)(2,1)S(1)}, bf16[64,2048]{1,0:T(8,128)(2,1)S(1)}, u32[]{:S(2)}, u32[]{:S(2)}) collective-permute-start(bf16[64,2048]{1,0:T(8,128)(2,1)S(1)} %collective-permute-done.6.refs_1_), channel_id=1, source_target_pairs={{0,1},{1,0},{2,3},{3,2},{4,5},{5,4},{6,7},{7,6},{8,9},{9,8},{10,11... | collective-permute-start | bytes 786440 | tf_op jit(solution)/shard_map/grads_across/ppermute | solution.py:445
  37.4 10.2 %collective-permute-start.8 = (bf16[64,2048]{1,0:T(8,128)(2,1)S(1)}, bf16[64,2048]{1,0:T(8,128)(2,1)S(1)}, u32[]{:S(2)}, u32[]{:S(2)}) collective-permute-start(bf16[64,2048]{1,0:T(8,128)(2,1)S(1)} %collective-permute-done.6.refs_1_), channel_id=1, source_target_pairs={{0,4},{2,6},{4,0},{6,2},{8,12},{10,14},{12,8},{14,10},{1,5},{3,7},... | collective-permute-start | bytes 786440 | tf_op jit(solution)/shard_map/grads_line/ppermute | solution.py:437
  37.7 21.2 %collective-permute-start.12 = (bf16[128,2048]{1,0:T(8,128)(2,1)S(1)}, bf16[128,2048]{1,0:T(8,128)(2,1)S(1)}, u32[]{:S(2)}, u32[]{:S(2)}) collective-permute-start(bf16[128,2048]{1,0:T(8,128)(2,1)S(1)} %get-tuple-element.259.refs_0_), channel_id=1, source_target_pairs={{0,4},{2,6},{4,0},{6,2},{8,12},{10,14},{12,8},{14,10},{1,5},{3,7},... | collective-permute-start | bytes 1572872 | tf_op jit(solution)/shard_map/grads_line/ppermute | solution.py:437
  42.4 7.2 %collective-permute-start.7 = (bf16[384,2176]{1,0:T(8,128)(2,1)S(1)}, bf16[384,2176]{1,0:T(8,128)(2,1)S(1)}, u32[]{:S(2)}, u32[]{:S(2)}) collective-permute-start(bf16[384,2176]{1,0:T(8,128)(2,1)S(1)} %join.4.refs_1_.refs_3_), channel_id=1, source_target_pairs={{0,2},{2,0},{4,6},{6,4},{8,10},{10,8},{12,14},{14,12},{1,3},{3,1},... | collective-permute-start | bytes 5013512 | tf_op jit(solution)/shard_map/rows_cores/ppermute | solution.py:441
  47.0 11.9 %collective-permute-start.14 = (bf16[128,2048]{1,0:T(8,128)(2,1)S(1)}, bf16[128,2048]{1,0:T(8,128)(2,1)S(1)}, u32[]{:S(2)}, u32[]{:S(2)}) collective-permute-start(bf16[128,2048]{1,0:T(8,128)(2,1)S(1)} %get-tuple-element.259.refs_0_), channel_id=1, source_target_pairs={{0,2},{2,0},{4,6},{6,4},{8,10},{10,8},{12,14},{14,12},{1,3},{3,1},... | collective-permute-start | bytes 1572872 | tf_op jit(solution)/shard_map/grads_cores/ppermute | solution.py:441
  47.5 11.4 %collective-permute-start.13 = (bf16[64,2048]{1,0:T(8,128)(2,1)S(1)}, bf16[64,2048]{1,0:T(8,128)(2,1)S(1)}, u32[]{:S(2)}, u32[]{:S(2)}) collective-permute-start(bf16[64,2048]{1,0:T(8,128)(2,1)S(1)} %collective-permute-done.8.refs_4_), channel_id=1, source_target_pairs={{0,1},{1,0},{2,3},{3,2},{4,5},{5,4},{6,7},{7,6},{8,9},{9,8},{10,11... | collective-permute-start | bytes 786440 | tf_op jit(solution)/shard_map/grads_across/ppermute | solution.py:445
  56.5 2.7 %collective-permute-start.11 = (bf16[512,1024]{1,0:T(8,128)(2,1)S(1)}, bf16[512,1024]{1,0:T(8,128)(2,1)S(1)}, u32[]{:S(2)}, u32[]{:S(2)}) collective-permute-start(bf16[512,1024]{1,0:T(8,128)(2,1)S(1)} %get-tuple-element.201), channel_id=1, source_target_pairs={{0,2},{2,0},{4,6},{6,4},{8,10},{10,8},{12,14},{14,12},{1,3},{3,1},... | collective-permute-start | bytes 3145736 | tf_op jit(solution)/shard_map/out_cores/ppermute | solution.py:441
  59.4 3.9 %collective-permute-start.15 = (bf16[384,2048]{1,0:T(8,128)(2,1)S(1)}, bf16[384,2048]{1,0:T(8,128)(2,1)S(1)}, u32[]{:S(2)}, u32[]{:S(2)}) collective-permute-start(bf16[384,2048]{1,0:T(8,128)(2,1)S(1)} %join.5.refs_1_), channel_id=1, source_target_pairs={{0,2},{2,0},{4,6},{6,4},{8,10},{10,8},{12,14},{14,12},{1,3},{3,1},... | collective-permute-start | bytes 4718600 | tf_op jit(solution)/shard_map/grads_cores/ppermute | solution.py:441
  59.7 20.3 %collective-permute-start.10 = (bf16[512,1024]{1,0:T(8,128)(2,1)S(1)}, bf16[512,1024]{1,0:T(8,128)(2,1)S(1)}, u32[]{:S(2)}, u32[]{:S(2)}) collective-permute-start(bf16[512,1024]{1,0:T(8,128)(2,1)S(1)} %get-tuple-element.202), channel_id=1, source_target_pairs={{0,2},{2,0},{4,6},{6,4},{8,10},{10,8},{12,14},{14,12},{1,3},{3,1},... | collective-permute-start | bytes 3145736 | tf_op jit(solution)/shard_map/out_cores/ppermute | solution.py:441
  60.0 20.1 %collective-permute-start.19 = (bf16[384,1024]{1,0:T(8,128)(2,1)S(1)}, bf16[384,1024]{1,0:T(8,128)(2,1)S(1)}, u32[]{:S(2)}, u32[]{:S(2)}) collective-permute-start(bf16[384,1024]{1,0:T(8,128)(2,1)S(1)} %get-tuple-element.214), channel_id=1, source_target_pairs={{0,1},{1,0},{2,3},{3,2},{4,5},{5,4},{6,7},{7,6},{8,9},{9,8},{10,11... | collective-permute-start | bytes 2359304 | tf_op jit(solution)/shard_map/out_across/ppermute | solution.py:445
  71.0 5.1 %collective-permute-start.17 = (bf16[256,1152]{1,0:T(8,128)(2,1)S(1)}, bf16[256,1152]{1,0:T(8,128)(2,1)S(1)}, u32[]{:S(2)}, u32[]{:S(2)}) collective-permute-start(bf16[256,1152]{1,0:T(8,128)(2,1)S(1)} %get-tuple-element.243), channel_id=1, source_target_pairs={{0,2},{2,0},{4,6},{6,4},{8,10},{10,8},{12,14},{14,12},{1,3},{3,1},... | collective-permute-start | bytes 1769480 | tf_op jit(solution)/shard_map/in_cores/ppermute | solution.py:441
  71.4 24.4 %collective-permute-start.16 = (bf16[256,1152]{1,0:T(8,128)(2,1)S(1)}, bf16[256,1152]{1,0:T(8,128)(2,1)S(1)}, u32[]{:S(2)}, u32[]{:S(2)}) collective-permute-start(bf16[256,1152]{1,0:T(8,128)(2,1)S(1)} %get-tuple-element.245), channel_id=1, source_target_pairs={{0,2},{2,0},{4,6},{6,4},{8,10},{10,8},{12,14},{14,12},{1,3},{3,1},... | collective-permute-start | bytes 1769480 | tf_op jit(solution)/shard_map/in_cores/ppermute | solution.py:441
  76.2 19.5 %collective-permute-start.18 = (bf16[256,1152]{1,0:T(8,128)(2,1)S(1)}, bf16[256,1152]{1,0:T(8,128)(2,1)S(1)}, u32[]{:S(2)}, u32[]{:S(2)}) collective-permute-start(bf16[256,1152]{1,0:T(8,128)(2,1)S(1)} %in_send.2), channel_id=1, source_target_pairs={{0,1},{1,0},{2,3},{3,2},{4,5},{5,4},{6,7},{7,6},{8,9},{9,8},{10,11... | collective-permute-start | bytes 1769480 | tf_op jit(solution)/shard_map/in_across/ppermute | solution.py:445
  78.3 18.7 %collective-permute-start.24 = (bf16[256,1152]{1,0:T(8,128)(2,1)S(1)}, bf16[256,1152]{1,0:T(8,128)(2,1)S(1)}, u32[]{:S(2)}, u32[]{:S(2)}) collective-permute-start(bf16[256,1152]{1,0:T(8,128)(2,1)S(1)} %get-tuple-element.242), channel_id=1, source_target_pairs={{0,2},{2,0},{4,6},{6,4},{8,10},{10,8},{12,14},{14,12},{1,3},{3,1},... | collective-permute-start | bytes 1769480 | tf_op jit(solution)/shard_map/in_cores/ppermute | solution.py:441
  80.4 13.0 %collective-permute-start.20 = (bf16[256,1024]{1,0:T(8,128)(2,1)S(1)}, bf16[256,1024]{1,0:T(8,128)(2,1)S(1)}, u32[]{:S(2)}, u32[]{:S(2)}) collective-permute-start(bf16[256,1024]{1,0:T(8,128)(2,1)S(1)} %get-tuple-element.258), channel_id=1, source_target_pairs={{0,4},{2,6},{4,0},{6,2},{8,12},{10,14},{12,8},{14,10},{1,5},{3,7},... | collective-permute-start | bytes 1572872 | tf_op jit(solution)/shard_map/out_line/ppermute | solution.py:437
  80.5 30.0 %collective-permute-start.23 = (bf16[256,1152]{1,0:T(8,128)(2,1)S(1)}, bf16[256,1152]{1,0:T(8,128)(2,1)S(1)}, u32[]{:S(2)}, u32[]{:S(2)}) collective-permute-start(bf16[256,1152]{1,0:T(8,128)(2,1)S(1)} %get-tuple-element.244), channel_id=1, source_target_pairs={{0,2},{2,0},{4,6},{6,4},{8,10},{10,8},{12,14},{14,12},{1,3},{3,1},... | collective-permute-start | bytes 1769480 | tf_op jit(solution)/shard_map/in_cores/ppermute | solution.py:441
  93.4 18.0 %collective-permute-start.22 = (bf16[128,1024]{1,0:T(8,128)(2,1)S(1)}, bf16[128,1024]{1,0:T(8,128)(2,1)S(1)}, u32[]{:S(2)}, u32[]{:S(2)}) collective-permute-start(bf16[128,1024]{1,0:T(8,128)(2,1)S(1)} %add_last.1), channel_id=1, source_target_pairs={{0,8},{2,10},{4,12},{6,14},{8,0},{10,2},{12,4},{14,6},{1,9},{3,11}... | collective-permute-start | bytes 786440 | tf_op jit(solution)/shard_map/out_line/ppermute | solution.py:437
  95.8 14.4 %collective-permute-start.26 = (bf16[128,1152]{1,0:T(8,128)(2,1)S(1)}, bf16[128,1152]{1,0:T(8,128)(2,1)S(1)}, u32[]{:S(2)}, u32[]{:S(2)}) collective-permute-start(bf16[128,1152]{1,0:T(8,128)(2,1)S(1)} %in_slot.3), channel_id=1, source_target_pairs={{0,4},{2,6},{4,0},{6,2},{8,12},{10,14},{12,8},{14,10},{1,5},{3,7},... | collective-permute-start | bytes 884744 | tf_op jit(solution)/shard_map/in_line/ppermute | solution.py:437
  97.1 13.4 %collective-permute-start.25 = (bf16[128,1152]{1,0:T(8,128)(2,1)S(1)}, bf16[128,1152]{1,0:T(8,128)(2,1)S(1)}, u32[]{:S(2)}, u32[]{:S(2)}) collective-permute-start(bf16[128,1152]{1,0:T(8,128)(2,1)S(1)} %get-tuple-element.273), channel_id=1, source_target_pairs={{0,1},{1,0},{2,3},{3,2},{4,5},{5,4},{6,7},{7,6},{8,9},{9,8},{10,11... | collective-permute-start | bytes 884744 | tf_op jit(solution)/shard_map/in_across/ppermute | solution.py:445
  97.7 12.8 %collective-permute-start.21 = (bf16[128,1024]{1,0:T(8,128)(2,1)S(1)}, bf16[128,1024]{1,0:T(8,128)(2,1)S(1)}, u32[]{:S(2)}, u32[]{:S(2)}) collective-permute-start(bf16[128,1024]{1,0:T(8,128)(2,1)S(1)} %get-tuple-element.270), channel_id=1, source_target_pairs={{0,1},{1,0},{2,3},{3,2},{4,5},{5,4},{6,7},{7,6},{8,9},{9,8},{10,11... | collective-permute-start | bytes 786440 | tf_op jit(solution)/shard_map/out_across/ppermute | solution.py:445
  110.4 10.5 %collective-permute-start.27 = (bf16[128,1152]{1,0:T(8,128)(2,1)S(1)}, bf16[128,1152]{1,0:T(8,128)(2,1)S(1)}, u32[]{:S(2)}, u32[]{:S(2)}) collective-permute-start(bf16[128,1152]{1,0:T(8,128)(2,1)S(1)} %in_slot.4), channel_id=1, source_target_pairs={{0,8},{2,10},{4,12},{6,14},{8,0},{10,2},{12,4},{14,6},{1,9},{3,11}... | collective-permute-start | bytes 884744 | tf_op jit(solution)/shard_map/in_line/ppermute | solution.py:437
  110.6 10.3 %collective-permute-start.29 = (bf16[128,1152]{1,0:T(8,128)(2,1)S(1)}, bf16[128,1152]{1,0:T(8,128)(2,1)S(1)}, u32[]{:S(2)}, u32[]{:S(2)}) collective-permute-start(bf16[128,1152]{1,0:T(8,128)(2,1)S(1)} %get-tuple-element.302), channel_id=1, source_target_pairs={{0,1},{1,0},{2,3},{3,2},{4,5},{5,4},{6,7},{7,6},{8,9},{9,8},{10,11... | collective-permute-start | bytes 884744 | tf_op jit(solution)/shard_map/in_across/ppermute | solution.py:445
  111.2 9.9 %collective-permute-start.28 = (bf16[128,1152]{1,0:T(8,128)(2,1)S(1)}, bf16[128,1152]{1,0:T(8,128)(2,1)S(1)}, u32[]{:S(2)}, u32[]{:S(2)}) collective-permute-start(bf16[128,1152]{1,0:T(8,128)(2,1)S(1)} %in_slot.5), channel_id=1, source_target_pairs={{0,4},{2,6},{4,0},{6,2},{8,12},{10,14},{12,8},{14,10},{1,5},{3,7},... | collective-permute-start | bytes 884744 | tf_op jit(solution)/shard_map/in_line/ppermute | solution.py:437
  118.5 2.7 %copy-start.1 = (s32[128,4]{0,1:T(4,128)S(1)}, s32[128,4]{0,1:T(4,128)}, u32[]{:S(2)}) copy-start(s32[128,4]{0,1:T(4,128)} %param.9) | copy-start | bytes 6148
  118.5 2.7 %copy-start.2 = (f32[128,4]{0,1:T(4,128)S(1)}, f32[128,4]{0,1:T(4,128)}, u32[]{:S(2)}) copy-start(f32[128,4]{0,1:T(4,128)} %param.11) | copy-start | bytes 6148
  118.5 2.6 %copy-start.3 = (s32[128]{0:T(128)S(1)}, s32[128]{0:T(128)}, u32[]{:S(2)}) copy-start(s32[128]{0:T(128)} %param.10) | copy-start | bytes 1540
